TPU v7x, 32 devices: a whole 2x2x4 slice. The times are simulated.
32 devices in a mesh: bucket: 2 (over x), blk: 16 (over z, y, core).
Axes of the slice: x: 2, y: 2, z: 4, core: 2. Of those that a mesh axis runs over, the one named last changes fastest.
Arguments:
- tokens: bfloat16 [2, 2, 2048, 1152], P('bucket', None, 'blk'), may hold values from -6 to 6
- cotangent: bfloat16 [2, 2, 2048, 1152], P('bucket', None, 'blk'), may hold values from -6 to 6
- doc_lengths: int32 [2, 2, 4], P('bucket'), may hold values from 1 to 1088, as said below
- w_query: bfloat16 [1152, 1024], P(('bucket', 'blk')), may hold values from -0.1875 to 0.1875
- w_key: bfloat16 [1152, 256], P(('bucket', 'blk')), may hold values from -0.1875 to 0.1875
- w_value: bfloat16 [1152, 256], P(('bucket', 'blk')), may hold values from -0.1875 to 0.1875
- w_out: bfloat16 [1024, 1152], P(('bucket', 'blk')), may hold values from -0.1875 to 0.1875
- w_gate: bfloat16 [1152, 6912], P(('bucket', 'blk')), may hold values from -0.1875 to 0.1875
- w_up: bfloat16 [1152, 6912], P(('bucket', 'blk')), may hold values from -0.1875 to 0.1875
- w_down: bfloat16 [6912, 1152], P(('bucket', 'blk')), may hold values from -0.078125 to 0.078125
- g_input: bfloat16 [1152], P(('bucket', 'blk')), may hold values from 0.5 to 1.5
- g_query: bfloat16 [256], P(('bucket', 'blk')), may hold values from -0.8984375 to 0.8984375
- g_key: bfloat16 [256], P(('bucket', 'blk')), may hold values from -0.8984375 to 0.8984375
- g_post_attn: bfloat16 [1152], P(('bucket', 'blk')), may hold values from 0.5 to 1.5
- g_pre_ffn: bfloat16 [1152], P(('bucket', 'blk')), may hold values from 0.5 to 1.5
- g_post_ffn: bfloat16 [1152], P(('bucket', 'blk')), may hold values from -0.8984375 to 0.8984375
Outputs:
- outputs: bfloat16 [2, 2, 2048, 1152], P('bucket', None, 'blk')
- input_grad: bfloat16 [2, 2, 2048, 1152], P('bucket', None, 'blk')
- grad_query: float32 [1152, 1024], P(('bucket', 'blk'))
- grad_key: float32 [1152, 256], P(('bucket', 'blk'))
- grad_value: float32 [1152, 256], P(('bucket', 'blk'))
- grad_out: float32 [1024, 1152], P(('bucket', 'blk'))
- grad_gate: float32 [1152, 6912], P(('bucket', 'blk'))
- grad_up: float32 [1152, 6912], P(('bucket', 'blk'))
- grad_down: float32 [6912, 1152], P(('bucket', 'blk'))
- grad_g_input: float32 [1152], P(('bucket', 'blk'))
- grad_g_query: float32 [256], P(('bucket', 'blk'))
- grad_g_key: float32 [256], P(('bucket', 'blk'))
- grad_g_post_attn: float32 [1152], P(('bucket', 'blk'))
- grad_g_pre_ffn: float32 [1152], P(('bucket', 'blk'))
- grad_g_post_ffn: float32 [1152], P(('bucket', 'blk'))
Inputs may be any that keep to these rules, and one draw needn't show every extreme that they name: `doc_lengths`: the first document of every bucket and micro-batch has exactly 1088 positions; the other 3 lengths add up to 960.
All inputs are finite; a program needn't handle non-finite values.
Results may differ from a plain program's by a relative error of at most 0.029.
Values may be sent and summed in bfloat16 or wider, within the bound.
A program may use at most 320 MiB of HBM per device.

v0:
```python
import jax
import jax.numpy as jnp
from jax import lax
from jax.sharding import PartitionSpec as P

H = 4
HD = 256


epsilon = 1e-06


def shifted(block, axis, distance):
    devices = range(lax.axis_size(axis))
    route = [(i - distance, i) for i in devices if i - distance in devices]
    return lax.ppermute(block, axis, route)


def from_behind(x, axis, by):
    devices = lax.axis_size(axis)
    return lax.ppermute(x, axis, [(i, (i + by) % devices) for i in range(devices)])


def scaled_norm(values, gain):
    return (
        values
        * lax.rsqrt(jnp.mean(values * values, axis=-1, keepdims=True) + epsilon)
        * (1.0 + gain)
    )


def segment_place(lengths, index_all):
    endings = jnp.cumsum(lengths, dtype=jnp.int32)
    before = index_all[:, None] >= endings[None, :]
    segment = jnp.sum(before.astype(jnp.int32), axis=1, dtype=jnp.int32)
    start_at = jnp.sum(jnp.where(before, lengths[None, :], 0), axis=1, dtype=jnp.int32)
    return (segment, index_all - start_at)


def rotate(values, position):
    halfway = values.shape[-1] // 2
    frequency = 1000000.0 ** (-(jnp.arange(halfway, dtype=jnp.float32) * 2.0 / values.shape[-1]))
    angles = position.astype(jnp.float32)[:, None] * frequency[None, :]
    if values.ndim == 3:
        angles = angles[:, None, :]
    cosine = jnp.cos(angles)
    sine_part = jnp.sin(angles)
    first_half = values[..., :halfway]
    second_half = values[..., halfway:]
    return jnp.concatenate(
        [
            first_half * cosine - second_half * sine_part,
            second_half * cosine + first_half * sine_part,
        ],
        axis=-1,
    )


def fetch(
    w_query,
    w_key,
    w_value,
    w_out,
    w_gate,
    w_up,
    w_down,
    g_input,
    g_query,
    g_key,
    g_post_attn,
    g_pre_ffn,
    g_post_ffn,
):
    return (
        lax.all_gather(w_query, ("bucket", "blk"), axis=0, tiled=True),
        lax.all_gather(w_key, ("bucket", "blk"), axis=0, tiled=True),
        lax.all_gather(w_value, ("bucket", "blk"), axis=0, tiled=True),
        lax.all_gather(w_out, ("bucket", "blk"), axis=0, tiled=True),
        lax.all_gather(w_gate, ("bucket", "blk"), axis=0, tiled=True),
        lax.all_gather(w_up, ("bucket", "blk"), axis=0, tiled=True),
        lax.all_gather(w_down, ("bucket", "blk"), axis=0, tiled=True),
        lax.all_gather(g_input, ("bucket", "blk"), axis=0, tiled=True),
        lax.all_gather(g_query, ("bucket", "blk"), axis=0, tiled=True),
        lax.all_gather(g_key, ("bucket", "blk"), axis=0, tiled=True),
        lax.all_gather(g_post_attn, ("bucket", "blk"), axis=0, tiled=True),
        lax.all_gather(g_pre_ffn, ("bucket", "blk"), axis=0, tiled=True),
        lax.all_gather(g_post_ffn, ("bucket", "blk"), axis=0, tiled=True),
    )


def allowed_mask(lengths, query_seg, query_index, anchor, row_count):
    key_index = anchor * row_count + jnp.arange(row_count, dtype=jnp.int32)
    key_seg, key_place = segment_place(lengths, key_index)
    return (
        (query_seg[:, None] == key_seg[None, :]) & (key_index[None, :] <= query_index[:, None])
    )[None]


def absorb(run_state, keys_blk, values_blk, anchor, queries, lengths, query_seg, query_index):
    row_count = queries.shape[0]
    score_scale = queries.shape[2] ** (-0.5)
    run_max, run_sum, accumulated = run_state
    allowed = allowed_mask(lengths, query_seg, query_index, anchor, row_count)
    scores = (
        jnp.einsum("qhd,kd->hqk", queries, keys_blk, preferred_element_type=jnp.float32)
        * score_scale
    )
    scores = jnp.where(allowed, scores, -1e30)
    new_max = jnp.maximum(run_max, jnp.max(scores, axis=-1))
    exp_terms = jnp.where(allowed, jnp.exp(scores - new_max[:, :, None]), 0.0)
    rescale = jnp.exp(run_max - new_max)
    run_sum = run_sum * rescale + jnp.sum(exp_terms, axis=-1)
    accumulated = accumulated * rescale.T[:, :, None] + jnp.einsum(
        "hqk,kd->qhd",
        exp_terms.astype(jnp.bfloat16),
        values_blk,
        preferred_element_type=jnp.float32,
    )
    return (new_max, run_sum, accumulated)


def contribute(
    keys_blk,
    values_blk,
    d_keys_blk,
    d_values_blk,
    d_queries,
    anchor,
    queries,
    d_attended,
    log_total,
    row_delta,
    lengths,
    query_seg,
    query_index,
):
    row_count = queries.shape[0]
    score_scale = queries.shape[2] ** (-0.5)
    allowed = allowed_mask(lengths, query_seg, query_index, anchor, row_count)
    scores = (
        jnp.einsum("qhd,kd->hqk", queries, keys_blk, preferred_element_type=jnp.float32)
        * score_scale
    )
    probability = jnp.where(allowed, jnp.exp(scores - log_total[:, :, None]), 0.0)
    prob_bf = probability.astype(jnp.bfloat16)
    d_values_blk = d_values_blk + jnp.einsum(
        "hqk,qhd->kd", prob_bf, d_attended, preferred_element_type=jnp.float32
    )
    d_probs = jnp.einsum("qhd,kd->hqk", d_attended, values_blk, preferred_element_type=jnp.float32)
    d_scores = (probability * (d_probs - row_delta[:, :, None])).astype(jnp.bfloat16)
    d_queries = (
        d_queries
        + jnp.einsum("hqk,kd->qhd", d_scores, keys_blk, preferred_element_type=jnp.float32)
        * score_scale
    )
    d_keys_blk = (
        d_keys_blk
        + jnp.einsum("hqk,qhd->kd", d_scores, queries, preferred_element_type=jnp.float32)
        * score_scale
    )
    return (d_keys_blk, d_values_blk, d_queries)


def start_state(queries):
    head_count = queries.shape[1]
    row_count = queries.shape[0]
    return (
        jnp.full((head_count, row_count), -1e30, jnp.float32),
        jnp.zeros((head_count, row_count), jnp.float32),
        jnp.zeros(queries.shape, jnp.float32),
    )


def finish_state(run_state):
    run_max, run_sum, accumulated = run_state
    return (accumulated / run_sum.T[:, :, None], run_max + jnp.log(run_sum))


def forward_cycle(
    queries, keys_own, values_own, lengths, query_seg, query_index, me_index, cycle_size
):

    def forward_turn(turn_index, carry):
        run_state, keys_blk, values_blk = carry
        anchor = jnp.remainder(me_index - turn_index, cycle_size)
        run_state = absorb(
            run_state, keys_blk, values_blk, anchor, queries, lengths, query_seg, query_index
        )
        keys_blk, values_blk = shifted((keys_blk, values_blk), "blk", 1)
        return (run_state, keys_blk, values_blk)

    run_state, keys_blk, values_blk = lax.fori_loop(
        0, cycle_size - 1, forward_turn, (start_state(queries), keys_own, values_own)
    )
    anchor = jnp.remainder(me_index - (cycle_size - 1), cycle_size)
    run_state = absorb(
        run_state, keys_blk, values_blk, anchor, queries, lengths, query_seg, query_index
    )
    return finish_state(run_state)


def backward_cycle(
    queries,
    keys_own,
    values_own,
    d_attended,
    log_total,
    row_delta,
    lengths,
    query_seg,
    query_index,
    me_index,
    cycle_size,
):

    def pass_grads(d_keys_blk, d_values_blk):
        return (
            from_behind(d_keys_blk.astype(jnp.bfloat16), "blk", 1).astype(d_keys_blk.dtype),
            from_behind(d_values_blk.astype(jnp.bfloat16), "blk", 1).astype(d_values_blk.dtype),
        )

    def backward_turn(turn_index, carry):
        keys_blk, values_blk, d_keys_blk, d_values_blk, d_queries = carry
        anchor = jnp.remainder(me_index - turn_index, cycle_size)
        d_keys_blk, d_values_blk, d_queries = contribute(
            keys_blk,
            values_blk,
            d_keys_blk,
            d_values_blk,
            d_queries,
            anchor,
            queries,
            d_attended,
            log_total,
            row_delta,
            lengths,
            query_seg,
            query_index,
        )
        keys_blk, values_blk = shifted((keys_blk, values_blk), "blk", 1)
        d_keys_blk, d_values_blk = pass_grads(d_keys_blk, d_values_blk)
        return (keys_blk, values_blk, d_keys_blk, d_values_blk, d_queries)

    zero_keys = jnp.zeros(keys_own.shape, jnp.float32)
    start_carry = (
        keys_own,
        values_own,
        zero_keys,
        zero_keys,
        jnp.zeros(queries.shape, jnp.float32),
    )
    keys_blk, values_blk, d_keys_blk, d_values_blk, d_queries = lax.fori_loop(
        0, cycle_size - 1, backward_turn, start_carry
    )
    anchor = jnp.remainder(me_index - (cycle_size - 1), cycle_size)
    d_keys_blk, d_values_blk, d_queries = contribute(
        keys_blk,
        values_blk,
        d_keys_blk,
        d_values_blk,
        d_queries,
        anchor,
        queries,
        d_attended,
        log_total,
        row_delta,
        lengths,
        query_seg,
        query_index,
    )
    d_keys_blk, d_values_blk = pass_grads(d_keys_blk, d_values_blk)
    return (d_queries, d_keys_blk, d_values_blk)


def middle(attn_value, x_value, gain_attn, gain_pre):
    hidden = x_value + scaled_norm(attn_value, gain_attn)
    return (hidden, scaled_norm(hidden, gain_pre))


def activate(gate_value, up_value):
    return jax.nn.gelu(gate_value, approximate=True) * up_value


def shards(
    tokens,
    cotangent,
    doc_lengths,
    w_query,
    w_key,
    w_value,
    w_out,
    w_gate,
    w_up,
    w_down,
    g_input,
    g_query,
    g_key,
    g_post_attn,
    g_pre_ffn,
    g_post_ffn,
):
    micro_count = tokens.shape[1]
    row_count = tokens.shape[2]
    cycle_size = lax.axis_size("blk")
    me_index = lax.axis_index("blk")
    spread = lax.axis_size(("bucket", "blk"))
    query_index = me_index * row_count + jnp.arange(row_count, dtype=jnp.int32)
    shard_list = (
        w_query,
        w_key,
        w_value,
        w_out,
        w_gate,
        w_up,
        w_down,
        g_input,
        g_query,
        g_key,
        g_post_attn,
        g_pre_ffn,
        g_post_ffn,
    )
    totals = [
        jnp.zeros((piece.shape[0] * spread,) + piece.shape[1:], jnp.float32) for piece in shard_list
    ]
    outputs_all = []
    grads_in = []
    for micro_index in range(micro_count):
        gathered = fetch(
            w_query,
            w_key,
            w_value,
            w_out,
            w_gate,
            w_up,
            w_down,
            g_input,
            g_query,
            g_key,
            g_post_attn,
            g_pre_ffn,
            g_post_ffn,
        )
        wq_full, wk_full, wv_full, wo_full, wg_full, wu_full, wd_full = gathered[:7]
        gain_in, gain_query, gain_key, gain_attn, gain_pre, gain_post = [
            gain_now.astype(jnp.float32) for gain_now in gathered[7:]
        ]
        lengths = doc_lengths[0, micro_index]
        query_seg, query_place = segment_place(lengths, query_index)
        x_rows = tokens[0, micro_index].astype(jnp.float32)
        normed, pre_pull = jax.vjp(scaled_norm, x_rows, gain_in)
        normed_bf = normed.astype(jnp.bfloat16)
        query_raw = jnp.dot(normed_bf, wq_full, preferred_element_type=jnp.float32).reshape(
            row_count, H, HD
        )
        key_raw = jnp.dot(normed_bf, wk_full, preferred_element_type=jnp.float32)
        values_bf = jnp.dot(normed_bf, wv_full, preferred_element_type=jnp.float32).astype(
            jnp.bfloat16
        )

        def shape_heads(raw_value, gain_value):
            return rotate(scaled_norm(raw_value, gain_value), query_place)

        queries, query_pull = jax.vjp(shape_heads, query_raw, gain_query)
        keys_f, key_pull = jax.vjp(shape_heads, key_raw, gain_key)
        queries_bf = queries.astype(jnp.bfloat16)
        keys_bf = keys_f.astype(jnp.bfloat16)
        attended, log_total = forward_cycle(
            queries_bf, keys_bf, values_bf, lengths, query_seg, query_index, me_index, cycle_size
        )
        attended_bf = attended.astype(jnp.bfloat16).reshape(row_count, H * HD)
        attn_out = jnp.dot(attended_bf, wo_full, preferred_element_type=jnp.float32)
        (hidden, ffn_in), mid_pull = jax.vjp(middle, attn_out, x_rows, gain_attn, gain_pre)
        ffn_bf = ffn_in.astype(jnp.bfloat16)
        gate_proj = jnp.dot(ffn_bf, wg_full, preferred_element_type=jnp.float32)
        up_proj = jnp.dot(ffn_bf, wu_full, preferred_element_type=jnp.float32)
        product, act_pull = jax.vjp(activate, gate_proj, up_proj)
        product_bf = product.astype(jnp.bfloat16)
        down_out = jnp.dot(product_bf, wd_full, preferred_element_type=jnp.float32)
        branch, out_pull = jax.vjp(scaled_norm, down_out, gain_post)
        outputs_all.append((hidden + branch).astype(jnp.bfloat16))
        upstream = cotangent[0, micro_index].astype(jnp.float32)
        d_down, d_gain_post = out_pull(upstream)
        d_down_bf = d_down.astype(jnp.bfloat16)
        grad_down = jnp.einsum(
            "tf,td->fd", product_bf, d_down_bf, preferred_element_type=jnp.float32
        )
        d_product = jnp.einsum("td,fd->tf", d_down_bf, wd_full, preferred_element_type=jnp.float32)
        d_gate, d_up = act_pull(d_product)
        d_gate_bf = d_gate.astype(jnp.bfloat16)
        d_up_bf = d_up.astype(jnp.bfloat16)
        grad_gate = jnp.einsum("td,tf->df", ffn_bf, d_gate_bf, preferred_element_type=jnp.float32)
        grad_up = jnp.einsum("td,tf->df", ffn_bf, d_up_bf, preferred_element_type=jnp.float32)
        d_ffn = jnp.einsum(
            "tf,df->td", d_gate_bf, wg_full, preferred_element_type=jnp.float32
        ) + jnp.einsum("tf,df->td", d_up_bf, wu_full, preferred_element_type=jnp.float32)
        d_attn, d_x_mid, d_gain_attn, d_gain_pre = mid_pull((upstream, d_ffn))
        d_attn_bf = d_attn.astype(jnp.bfloat16)
        grad_out = jnp.einsum(
            "tc,td->cd", attended_bf, d_attn_bf, preferred_element_type=jnp.float32
        )
        d_attended = (
            jnp.einsum("td,cd->tc", d_attn_bf, wo_full, preferred_element_type=jnp.float32)
            .astype(jnp.bfloat16)
            .reshape(row_count, H, HD)
        )
        row_delta = jnp.sum(d_attended.astype(jnp.float32) * attended, axis=-1).T
        d_queries, d_keys, d_values = backward_cycle(
            queries_bf,
            keys_bf,
            values_bf,
            d_attended,
            log_total,
            row_delta,
            lengths,
            query_seg,
            query_index,
            me_index,
            cycle_size,
        )
        d_query_raw, d_gain_query = query_pull(d_queries)
        d_key_raw, d_gain_key = key_pull(d_keys)
        d_query_bf = d_query_raw.reshape(row_count, H * HD).astype(jnp.bfloat16)
        d_key_bf = d_key_raw.astype(jnp.bfloat16)
        d_value_bf = d_values.astype(jnp.bfloat16)
        grad_query = jnp.einsum(
            "td,tc->dc", normed_bf, d_query_bf, preferred_element_type=jnp.float32
        )
        grad_key = jnp.einsum("td,tc->dc", normed_bf, d_key_bf, preferred_element_type=jnp.float32)
        grad_value = jnp.einsum(
            "td,tc->dc", normed_bf, d_value_bf, preferred_element_type=jnp.float32
        )
        d_normed = jnp.einsum("tc,dc->td", d_query_bf, wq_full, preferred_element_type=jnp.float32)
        d_normed = d_normed + jnp.einsum(
            "tc,dc->td", d_key_bf, wk_full, preferred_element_type=jnp.float32
        )
        d_normed = d_normed + jnp.einsum(
            "tc,dc->td", d_value_bf, wv_full, preferred_element_type=jnp.float32
        )
        d_x_pre, d_gain_in = pre_pull(d_normed)
        grads_in.append((d_x_mid + d_x_pre).astype(jnp.bfloat16))
        pieces = (
            grad_query,
            grad_key,
            grad_value,
            grad_out,
            grad_gate,
            grad_up,
            grad_down,
            d_gain_in,
            d_gain_query,
            d_gain_key,
            d_gain_attn,
            d_gain_pre,
            d_gain_post,
        )
        totals = [total_now + piece_now for total_now, piece_now in zip(totals, pieces)]
    summed = (
        lax.psum_scatter(totals[0], ("bucket", "blk"), scatter_dimension=0, tiled=True),
        lax.psum_scatter(totals[1], ("bucket", "blk"), scatter_dimension=0, tiled=True),
        lax.psum_scatter(totals[2], ("bucket", "blk"), scatter_dimension=0, tiled=True),
        lax.psum_scatter(totals[3], ("bucket", "blk"), scatter_dimension=0, tiled=True),
        lax.psum_scatter(totals[4], ("bucket", "blk"), scatter_dimension=0, tiled=True),
        lax.psum_scatter(totals[5], ("bucket", "blk"), scatter_dimension=0, tiled=True),
        lax.psum_scatter(totals[6], ("bucket", "blk"), scatter_dimension=0, tiled=True),
        lax.psum_scatter(totals[7], ("bucket", "blk"), scatter_dimension=0, tiled=True),
        lax.psum_scatter(totals[8], ("bucket", "blk"), scatter_dimension=0, tiled=True),
        lax.psum_scatter(totals[9], ("bucket", "blk"), scatter_dimension=0, tiled=True),
        lax.psum_scatter(totals[10], ("bucket", "blk"), scatter_dimension=0, tiled=True),
        lax.psum_scatter(totals[11], ("bucket", "blk"), scatter_dimension=0, tiled=True),
        lax.psum_scatter(totals[12], ("bucket", "blk"), scatter_dimension=0, tiled=True),
    )
    return (jnp.stack(outputs_all)[None], jnp.stack(grads_in)[None]) + tuple(summed)


def solution(mesh):
    return jax.shard_map(
        shards,
        mesh=mesh,
        in_specs=(
            P("bucket", None, "blk", None),
            P("bucket", None, "blk", None),
            P("bucket", None, None),
            P(("bucket", "blk"), None),
            P(("bucket", "blk"), None),
            P(("bucket", "blk"), None),
            P(("bucket", "blk"), None),
            P(("bucket", "blk"), None),
            P(("bucket", "blk"), None),
            P(("bucket", "blk"), None),
            P(("bucket", "blk")),
            P(("bucket", "blk")),
            P(("bucket", "blk")),
            P(("bucket", "blk")),
            P(("bucket", "blk")),
            P(("bucket", "blk")),
        ),
        out_specs=(
            P("bucket", None, "blk", None),
            P("bucket", None, "blk", None),
            P(("bucket", "blk"), None),
            P(("bucket", "blk"), None),
            P(("bucket", "blk"), None),
            P(("bucket", "blk"), None),
            P(("bucket", "blk"), None),
            P(("bucket", "blk"), None),
            P(("bucket", "blk"), None),
            P(("bucket", "blk")),
            P(("bucket", "blk")),
            P(("bucket", "blk")),
            P(("bucket", "blk")),
            P(("bucket", "blk")),
            P(("bucket", "blk")),
        ),
        check_vma=False,
    )
```

profile of v0, /device:TPU:7, one launch (start us, length us, event | category | flops | bytes accessed | tf_op | source)
XLA Modules:
  0.0 2411.8 jit_solution(520873083513186253)
XLA Ops:
  15.8 40.8 %all-reduce.32 = (bf16[1152]{0:T(1024)(128)(2,1)S(1)}, bf16[256]{0:T(256)(128)(2,1)S(1)}, bf16[256]{0:T(256)(128)(2,1)S(1)}, bf16[1152]{0:T(1024)(128)(2,1)}, bf...) all-reduce(bf16[1152]{0:T(1024)(128)(2,1)S(1)} %dynamic-update-slic, ...), channel_id=1, replica_groups=mesh['bucket'=2,'blk'=16] {'bucket','blk'}, use_global_device_ids=true, to_apply=%add.8 | all-reduce | flops 5120 | bytes 20480
  57.9 40.7 %all-gather = bf16[32,36,256]{2,1,0:T(8,128)(2,1)S(1)} all-gather(bf16[1,36,256]{2,1,0:T(8,128)(2,1)} %bitcast.613), channel_id=1, replica_groups=mesh['bucket'=2,'blk'=16] {'bucket','blk'}, dimensions={0}, use_global_device_ids=true | all-gather | bytes 608256 | tf_op jit(solution)/shard_map/all_gather | solution.py:76
  99.6 42.3 %all-gather.1 = bf16[32,36,256]{2,1,0:T(8,128)(2,1)S(1)} all-gather(bf16[1,36,256]{2,1,0:T(8,128)(2,1)S(1)} %bitcast.614), channel_id=1, replica_groups=mesh['bucket'=2,'blk'=16] {'bucket','blk'}, dimensions={0}, use_global_device_ids=true | all-gather | bytes 608256 | tf_op jit(solution)/shard_map/all_gather | solution.py:77
  166.2 154.3 %while.97 = (s32[]{:T(128)}, f32[4,128]{1,0:T(4,128)S(1)}, f32[4,128]{1,0:T(4,128)S(1)}, f32[128,4,256]{2,0,1:T(8,128)S(1)}, bf16[128,256]{1,0:T(8,128)(2,1)S(1)...) while((s32[]{:T(128)}, f32[4,128]{1,0:T(4,128)S(1)}, ...), condition=%wide.region_29.30_spmd.clone, body=%wide.region_25.29_spmd.clone.sunk | while | flops 68145808 | bytes 3117454 | solution.py:192
  321.6 172.7 %while.96 = (s32[]{:T(128)}, f32[4,128]{1,0:T(4,128)S(1)}, f32[4,128]{1,0:T(4,128)S(1)}, f32[128,4,256]{2,0,1:T(8,128)S(1)}, bf16[128,256]{1,0:T(8,128)(2,1)S(1)...) while((s32[]{:T(128)}, f32[4,128]{1,0:T(4,128)S(1)}, ...), condition=%wide.region_11.12_spmd.clone, body=%wide.region_7.11_spmd.clone.sunk | while | flops 68145808 | bytes 3117454 | solution.py:192
  507.2 18.6 reshape.988
  525.8 18.6 reshape.990
  605.1 13.4 fusion.291
  630.1 23.5 convolution_add_fusion
  653.6 372.7 %fusion.12 = f32[40,6912]{1,0:T(8,128)} fusion(f32[1152,6912]{1,0:T(8,128)} %convolution_add_fusion), kind=kCustom, calls=%all-reduce-scatter.4 | all-reduce-scatter fusion | flops 8847361 | bytes 32956416
  1030.0 12.0 fusion.285
  1065.1 13.0 multiply_reduce_fusion.1
  1097.6 269.9 %while.98 = (s32[]{:T(128)}, bf16[128,256]{1,0:T(8,128)(2,1)S(1)}, bf16[128,256]{1,0:T(8,128)(2,1)}, f32[128,256]{1,0:T(8,128)}, f32[128,256]{1,0:T(8,128)S(1)},...) while((s32[]{:T(128)}, bf16[128,256]{1,0:T(8,128)(2,1)S(1)}, ...), condition=%wide.region_42.43_spmd.clone, body=%wide.region_40.42_spmd.clone.sunk | while | flops 168969872 | bytes 5612022 | solution.py:252
  1121.0 17.5 collective-permute-start.4
  1369.7 13.6 fusion.292
  1383.3 23.5 convolution_add_fusion.2
  1408.0 212.2 %while.99 = (s32[]{:T(128)}, bf16[128,256]{1,0:T(8,128)(2,1)S(1)}, bf16[128,256]{1,0:T(8,128)(2,1)S(1)}, f32[128,256]{1,0:T(8,128)S(1)}, f32[128,256]{1,0:T(8,12...) while((s32[]{:T(128)}, bf16[128,256]{1,0:T(8,128)(2,1)S(1)}, ...), condition=%wide.region_52.53_spmd.clone, body=%wide.region_50.52_spmd.clone.sunk | while | flops 168969872 | bytes 5612022 | solution.py:252
  1643.3 12.9 fusion.290
  1656.3 24.1 convolution_add_fusion.1
  1690.0 473.4 %fusion.274 = (f32[40,1024]{1,0:T(8,128)}, f32[40,256]{1,0:T(8,128)}, f32[40,256]{1,0:T(8,128)}, f32[40,6912]{1,0:T(8,128)}) fusion(f32[1152,1024]{1,0:T(8,128)} %convolution_add_fusion.4, f32[1152,256]{1,0:T(8,128)S(1)} %convolution_add_fusion.6, f32[1152,256]{1,0:T(8,128)} %convolution_add_fusion.5, f32[1152,6912]{1,0:T(8,128)} %convolution_add_fusion.1), kind=kCustom, calls=%all-reduce-scatter.5 | all-reduce-scatter fusion | flops 10813441 | bytes 40280064
  2210.5 80.1 %all-reduce.31 = (f32[1152]{0:T(1024)S(1)}, f32[256]{0:T(256)S(1)}, f32[256]{0:T(256)S(1)}, f32[1152]{0:T(1024)S(1)}, f32[1152]{0:T(1024)S(1)}, /*index=5*/f32[1152]{0:T(1024)S(1)}) all-reduce(f32[1152]{0:T(1024)S(1)} %add.761, f32[256]{0:T(256)} %add.762, ...), channel_id=9, replica_groups=mesh['bucket'=2,'blk'=16] {'bucket','blk'}, use_global_device_ids=true, to_apply=%region_65.66.clone | all-reduce | flops 5120 | bytes 40960
  2335.8 23.7 concatenate.24
  2362.0 19.3 collective-permute-done.31
  2381.3 21.0 concatenate.23
  (1757 shorter events, 1082.1 us)
Async XLA Ops:
  7.2 146.3 %all-gather.15.cloned.1.call-start = ((), (), s32[]{:S(2)}) async-start(), calls=%async_computation.5 | async-start | bytes 2703360 | tf_op jit(solution)/shard_map/all_gather | solution.py:75
  7.9 491.3 %all-gather.11.cloned.1.call-start = ((), (), s32[]{:S(2)}) async-start(), calls=%async_computation.2 | async-start | bytes 2433024 | tf_op jit(solution)/shard_map/all_gather | solution.py:78
  8.7 498.5 %all-gather.17.cloned.1.call-start = ((), (), s32[]{:S(2)}) async-start(), calls=%async_computation.6 | async-start | bytes 18247680 | tf_op jit(solution)/shard_map/all_gather | solution.py:79
  9.4 516.4 %all-gather.19.cloned.1.call-start = ((), (), s32[]{:S(2)}) async-start(), calls=%async_computation.7 | async-start | bytes 18247680 | tf_op jit(solution)/shard_map/all_gather | solution.py:80
  10.0 551.0 %all-gather.13.cloned.1.call-start = ((), (), s32[]{:S(2)}) async-start(), calls=%async_computation.3 | async-start | bytes 16422912 | tf_op jit(solution)/shard_map/all_gather | solution.py:81
  10.6 2394.1 %reduce-scatter.15.cloned.1.call-start = ((), (), s32[]{:S(2)}) async-start(), calls=%async_computation.4 | async-start | bytes 4866048 | tf_op jit(solution)/shard_map/reduce_scatter | solution.py:462
  1026.3 1292.3 %collective-permute-start.32 = (f32[40,6912]{1,0:T(8,128)}, f32[40,6912]{1,0:T(8,128)}, u32[]{:S(2)}, u32[]{:S(2)}) collective-permute-start(f32[40,6912]{1,0:T(8,128)} %fusion.12), channel_id=1, source_target_pairs={{0,1},{1,2},{2,3},{3,4},{4,5},{5,6},{6,7},{7,8},{8,9},{9,10},{10,1... | collective-permute-start | bytes 3317768
  1096.7 1308.1 %reduce-scatter.17.cloned.1.call-start = ((), (), s32[]{:S(2)}) async-start(), calls=%async_computation.8 | async-start | bytes 32845824
  1097.6 23.3 collective-permute-start.4
  1121.0 32.6 %collective-permute-start.4 = (bf16[128,256]{1,0:T(8,128)(2,1)S(1)}, bf16[128,256]{1,0:T(8,128)(2,1)S(1)}, u32[]{:S(2)}, u32[]{:S(2)}) collective-permute-start(bf16[128,256]{1,0:T(8,128)(2,1)S(1)} %copy.208), channel_id=1, source_target_pairs={{0,1},{1,2},{2,3},{3,4},{4,5},{5,6},{6,7},{7,8},{8,9},{9,10},{10,1... | collective-permute-start | bytes 196616 | tf_op jit(solution)/shard_map/while/body/eval_jaxpr/ppermute | solution.py:16
  1620.3 67.4 %collective-permute-start.13 = (bf16[128,256]{1,0:T(8,128)(2,1)}, bf16[128,256]{1,0:T(8,128)(2,1)}, u32[]{:S(2)}, u32[]{:S(2)}) collective-permute-start(bf16[128,256]{1,0:T(8,128)(2,1)} %fusion.124), channel_id=1, source_target_pairs={{0,1},{1,2},{2,3},{3,4},{4,5},{5,6},{6,7},{7,8},{8,9},{9,10},{10,1... | collective-permute-start | bytes 196616 | tf_op jit(solution)/shard_map/ppermute | solution.py:21
  1630.4 52.8 %collective-permute-start.14 = (bf16[128,256]{1,0:T(8,128)(2,1)}, bf16[128,256]{1,0:T(8,128)(2,1)S(1)}, u32[]{:S(2)}, u32[]{:S(2)}) collective-permute-start(bf16[128,256]{1,0:T(8,128)(2,1)} %fusion.125), channel_id=1, source_target_pairs={{0,1},{1,2},{2,3},{3,4},{4,5},{5,6},{6,7},{7,8},{8,9},{9,10},{10,1... | collective-permute-start | bytes 196616 | tf_op jit(solution)/shard_map/ppermute | solution.py:21
  1632.4 50.7 %collective-permute-start.12 = (bf16[128,256]{1,0:T(8,128)(2,1)}, bf16[128,256]{1,0:T(8,128)(2,1)}, u32[]{:S(2)}, u32[]{:S(2)}) collective-permute-start(bf16[128,256]{1,0:T(8,128)(2,1)} %fusion.126), channel_id=1, source_target_pairs={{0,1},{1,2},{2,3},{3,4},{4,5},{5,6},{6,7},{7,8},{8,9},{9,10},{10,1... | collective-permute-start | bytes 196616 | tf_op jit(solution)/shard_map/ppermute | solution.py:21
  1634.3 52.1 %collective-permute-start.15 = (bf16[128,256]{1,0:T(8,128)(2,1)}, bf16[128,256]{1,0:T(8,128)(2,1)}, u32[]{:S(2)}, u32[]{:S(2)}) collective-permute-start(bf16[128,256]{1,0:T(8,128)(2,1)} %fusion.123), channel_id=1, source_target_pairs={{0,1},{1,2},{2,3},{3,4},{4,5},{5,6},{6,7},{7,8},{8,9},{9,10},{10,1... | collective-permute-start | bytes 196616 | tf_op jit(solution)/shard_map/ppermute | solution.py:21
  2163.4 33.0 %collective-permute-start.24 = (f32[40,256]{1,0:T(8,128)}, f32[40,256]{1,0:T(8,128)S(1)}, u32[]{:S(2)}, u32[]{:S(2)}) collective-permute-start(f32[40,256]{1,0:T(8,128)} %get-tuple-element.1693), channel_id=1, source_target_pairs={{0,1},{1,2},{2,3},{3,4},{4,5},{5,6},{6,7},{7,8},{8,9},{9,10},{10,1... | collective-permute-start | bytes 122888
  2165.5 32.9 %collective-permute-start.25 = (f32[40,256]{1,0:T(8,128)}, f32[40,256]{1,0:T(8,128)S(1)}, u32[]{:S(2)}, u32[]{:S(2)}) collective-permute-start(f32[40,256]{1,0:T(8,128)} %get-tuple-element.1693), channel_id=1, source_target_pairs={{0,2},{1,3},{2,4},{3,5},{4,6},{5,7},{6,8},{7,9},{8,10},{9,11},{10,... | collective-permute-start | bytes 122888
  2200.4 132.9 %collective-permute-start.33 = (f32[40,6912]{1,0:T(8,128)}, f32[40,6912]{1,0:T(8,128)}, u32[]{:S(2)}, u32[]{:S(2)}) collective-permute-start(f32[40,6912]{1,0:T(8,128)} %fusion.12), channel_id=1, source_target_pairs={{0,2},{1,3},{2,4},{3,5},{4,6},{5,7},{6,8},{7,9},{8,10},{9,11},{10,... | collective-permute-start | bytes 3317768
  2202.5 133.3 %collective-permute-start.34 = (f32[40,6912]{1,0:T(8,128)}, f32[40,6912]{1,0:T(8,128)}, u32[]{:S(2)}, u32[]{:S(2)}) collective-permute-start(f32[40,6912]{1,0:T(8,128)} %fusion.12), channel_id=1, source_target_pairs={{0,3},{1,4},{2,5},{3,6},{4,7},{5,8},{6,9},{7,10},{8,11},{9,12},{10... | collective-permute-start | bytes 3317768
  2204.7 90.0 %collective-permute-start.35 = (f32[4,6912]{1,0:T(4,128)}, f32[4,6912]{1,0:T(4,128)}, u32[]{:S(2)}, u32[]{:S(2)}) collective-permute-start(f32[4,6912]{1,0:T(4,128)} %slice.68), channel_id=1, source_target_pairs={{0,4},{1,5},{2,6},{3,7},{4,8},{5,9},{6,10},{7,11},{8,12},{9,13},{1... | collective-permute-start | bytes 331784
  2206.7 90.0 %collective-permute-start.16 = (f32[40,1024]{1,0:T(8,128)}, f32[40,1024]{1,0:T(8,128)}, u32[]{:S(2)}, u32[]{:S(2)}) collective-permute-start(f32[40,1024]{1,0:T(8,128)} %get-tuple-element.1691), channel_id=1, source_target_pairs={{0,1},{1,2},{2,3},{3,4},{4,5},{5,6},{6,7},{7,8},{8,9},{9,10},{10,1... | collective-permute-start | bytes 491528
  2313.6 67.7 %collective-permute-start.28 = (f32[40,6912]{1,0:T(8,128)S(1)}, f32[40,6912]{1,0:T(8,128)S(1)}, u32[]{:S(2)}, u32[]{:S(2)}) collective-permute-start(f32[40,6912]{1,0:T(8,128)S(1)} %copy-done.49), channel_id=1, source_target_pairs={{0,1},{1,2},{2,3},{3,4},{4,5},{5,6},{6,7},{7,8},{8,9},{9,10},{10,1... | collective-permute-start | bytes 3317768
  2315.5 65.8 %collective-permute-start.29 = (f32[40,6912]{1,0:T(8,128)S(1)}, f32[40,6912]{1,0:T(8,128)S(1)}, u32[]{:S(2)}, u32[]{:S(2)}) collective-permute-start(f32[40,6912]{1,0:T(8,128)S(1)} %copy-done.49), channel_id=1, source_target_pairs={{0,2},{1,3},{2,4},{3,5},{4,6},{5,7},{6,8},{7,9},{8,10},{9,11},{10,... | collective-permute-start | bytes 3317768
  2318.6 62.7 %collective-permute-start.30 = (f32[40,6912]{1,0:T(8,128)S(1)}, f32[40,6912]{1,0:T(8,128)}, u32[]{:S(2)}, u32[]{:S(2)}) collective-permute-start(f32[40,6912]{1,0:T(8,128)S(1)} %copy-done.49), channel_id=1, source_target_pairs={{0,3},{1,4},{2,5},{3,6},{4,7},{5,8},{6,9},{7,10},{8,11},{9,12},{10... | collective-permute-start | bytes 3317768
  2333.2 48.1 %collective-permute-start.31 = (f32[4,6912]{1,0:T(4,128)}, f32[4,6912]{1,0:T(4,128)S(1)}, u32[]{:S(2)}, u32[]{:S(2)}) collective-permute-start(f32[4,6912]{1,0:T(4,128)} %slice.67), channel_id=1, source_target_pairs={{0,4},{1,5},{2,6},{3,7},{4,8},{5,9},{6,10},{7,11},{8,12},{9,13},{1... | collective-permute-start | bytes 331784
  (384 other events, 8949.4 us)
Sparse Core Ops, SparseCore 0:
  10.9 58.9 all-gather.14
  72.8 55.7 all-gather.10
  131.5 124.4 all-gather.16
  258.7 125.5 all-gather.18
  387.0 116.7 all-gather.12
  1096.8 133.2 reduce-scatter.14
  1407.0 378.0 reduce-scatter.16
where the time goes:
time: 2430 us; the launch traced here: 2410 us
  blocking collectives  1050 us (43%)
  starting transfers between devices  612 us (25%)
  matrix products  388 us (16%)
  local copies, waits for them, and re-layouts  156 us (6%)
  other arithmetic  99.1 us (4%)
  waiting for transfers between devices  81.3 us (3%)
    unnamed x4, blocking collectives  967 us
    ppermute x120, starting transfers between devices, shifted(): return lax.ppermute(block, axis, route)  485 us
    unnamed x435, local copies, waits for them, and re-layouts  136 us
    ppermute x64, starting transfers between devices, from_behind(): lax.ppermute(x, axis, [(i, (i + by) % devices) for i in range(devices)])  71.4 us
    unnamed x21, starting transfers between devices  55.1 us
  transfers between devices with their start and end apart: 211, of which 54 were waited for; matrix products, arithmetic and copies ran while one was open for 42% of the time, Pallas kernels for 0%

commit v1 on v0

v1 whole, which is shorter than its diff:
```python
import functools
import math

import jax
import jax.numpy as jnp
from jax import lax
from jax.experimental import pallas as pl
from jax.experimental.pallas import tpu as pltpu
from jax.sharding import PartitionSpec as P

H = 4
HD = 256
F32 = jnp.float32
BF16 = jnp.bfloat16
MESH = pl.DeviceIdType.MESH
ANY = pl.BlockSpec(memory_space=pl.ANY)
VMEM = pl.BlockSpec(memory_space=pltpu.VMEM)
epsilon = 1e-06


def up16(n):
    return -(-n // 16) * 16


def place():
    b = lax.axis_index("bucket")
    k = lax.axis_index("blk")
    return b, k // 4, (k // 2) % 2, k % 2


def at(b, q, y, c):
    return (b, q * 4 + y * 2 + c)


def greet(targets):
    bar = pltpu.get_barrier_semaphore()
    for t in targets:
        pl.semaphore_signal(bar, inc=1, device_id=t, device_id_type=MESH)
    return bar


def remote(src, dst, send, recv, target):
    return pltpu.make_async_remote_copy(src, dst, send, recv, device_id=target, device_id_type=MESH)


def gather_kernel(nz, qkv, wo, gain, wg, wu, wd, qkv_f, wo_f, gain_f, wg_f, wu_f, wd_f, lsem, ssem, rsem, wls, wss, wrs):
    b, q, y, c = place()
    g, e = q // 2, q % 2
    ng = nz // 2
    qw = qkv.shape[1]
    self_in = e == c
    bar = greet(
        [at(b, lax.rem(q + r, nz), y, c) for r in range(1, nz)]
        + [at(1 - b, q, y, c), at(b, q, 1 - y, c), at(b, q, y, 1 - c)]
        + [at(b, lax.rem(g + r, ng) * 2 + c, y, e) for r in range(1, ng)]
    )
    first = at(b, g * 2 + c, y, e)

    @pl.when(jnp.logical_not(self_in))
    def _():
        pl.semaphore_signal(bar, inc=1, device_id=first, device_id_type=MESH)

    pl.semaphore_wait(bar, nz + 1 + ng - jnp.where(self_in, 1, 0) + 1)

    everything = pl.ds(0, nz)

    def view_qkv(ref, yy, cc, xx, qq):
        return ref.at[xx, qq, :, pl.ds(pl.multiple_of((yy * 2 + cc) * qw, 128), qw)]

    def view_lead(ref, yy, cc, xx, qq):
        return ref.at[xx, qq, yy, cc]

    items = [(qkv, qkv_f, view_qkv), (wo, wo_f, view_lead), (gain, gain_f, view_lead)]
    sent = []
    local = []
    for i, (src, dst, view) in enumerate(items):
        cp = pltpu.make_async_copy(src, view(dst, y, c, b, q), lsem.at[i])
        cp.start()
        local.append(cp)
    z_in = []
    for i, (src, dst, view) in enumerate(items):
        row = []
        for r in range(1, nz):
            cp = remote(src, view(dst, y, c, b, q), ssem.at[i, r], rsem.at[i, r], at(b, lax.rem(q + r, nz), y, c))
            cp.start()
            sent.append(cp)
            row.append(
                remote(src, view(dst, y, c, b, lax.rem(q - r + nz, nz)), ssem.at[i, r], rsem.at[i, r], at(b, lax.rem(q + r, nz), y, c))
            )
        z_in.append(row)
    x_in = [[] for _ in items]
    for i, (src, dst, view) in enumerate(items):
        cp = remote(src, view(dst, y, c, b, q), ssem.at[i, nz], rsem.at[i, nz], at(1 - b, q, y, c))
        cp.start()
        sent.append(cp)
        x_in[i].append(remote(src, view(dst, y, c, 1 - b, q), ssem.at[i, nz], rsem.at[i, nz], at(1 - b, q, y, c)))

    units = [(wg, wg_f), (wu, wu_f), (wd, wd_f)]
    u_in = []
    for j, (src, dst) in enumerate(units):
        row = []
        for r in range(ng):
            target = at(b, lax.rem(g + r, ng) * 2 + c, y, e)
            cp = remote(src, dst.at[b, q], wss.at[j, r], wrs.at[j, r], target)
            qs = lax.rem(g - r + ng, ng) * 2 + c
            inc = remote(src, dst.at[b, qs], wss.at[j, r], wrs.at[j, r], target)
            if r == 0:
                lc = pltpu.make_async_copy(src, dst.at[b, q], wls.at[j])

                @pl.when(self_in)
                def _():
                    lc.start()

                @pl.when(jnp.logical_not(self_in))
                def _():
                    cp.start()
            else:
                cp.start()
            row.append((cp, inc, qs, lc if r == 0 else None))
        u_in.append(row)

    for r in range(1, nz):
        qs = lax.rem(q - r + nz, nz)
        for i, (src, dst, view) in enumerate(items):
            z_in[i][r - 1].wait_recv()
            cp = remote(view(dst, y, c, b, qs), view(dst, y, c, b, qs), ssem.at[i, nz + r], rsem.at[i, nz + r], at(1 - b, q, y, c))
            cp.start()
            sent.append(cp)
            x_in[i].append(
                remote(view(dst, y, c, b, qs), view(dst, y, c, 1 - b, qs), ssem.at[i, nz + r], rsem.at[i, nz + r], at(1 - b, q, y, c))
            )
    for cp in local:
        cp.wait()
    y_in = [[] for _ in items]
    for half in range(2):
        for i, (src, dst, view) in enumerate(items):
            xx = b if half == 0 else 1 - b
            if half == 1:
                for cp in x_in[i]:
                    cp.wait_recv()
            s = 2 * nz + half
            cp = remote(view(dst, y, c, xx, everything), view(dst, y, c, xx, everything), ssem.at[i, s], rsem.at[i, s], at(b, q, 1 - y, c))
            cp.start()
            sent.append(cp)
            y_in[i].append(
                remote(view(dst, y, c, xx, everything), view(dst, 1 - y, c, xx, everything), ssem.at[i, s], rsem.at[i, s], at(b, q, 1 - y, c))
            )
    c_in = []

    def to_core(i, yy, s):
        _, dst, view = items[i]
        both = pl.ds(0, 2)
        cp = remote(view(dst, yy, c, both, everything), view(dst, yy, c, both, everything), ssem.at[i, s], rsem.at[i, s], at(b, q, y, 1 - c))
        cp.start()
        sent.append(cp)
        c_in.append(
            remote(view(dst, yy, c, both, everything), view(dst, yy, 1 - c, both, everything), ssem.at[i, s], rsem.at[i, s], at(b, q, y, 1 - c))
        )

    for i in range(len(items)):
        to_core(i, y, 2 * nz + 2)
    for i in range(len(items)):
        for cp in y_in[i]:
            cp.wait_recv()
        to_core(i, 1 - y, 2 * nz + 3)

    d_in = []

    def unit_on(j, xx, qs, s, target, yours):
        _, dst = units[j]
        cp = remote(dst.at[xx, qs], dst.at[xx, qs], wss.at[j, s], wrs.at[j, s], target)
        cp.start()
        sent.append(cp)
        return remote(dst.at[xx, qs], dst.at[yours[0], yours[1]], wss.at[j, s], wrs.at[j, s], target)

    xw = [[] for _ in units]

    def x_round(j):
        for r in range(ng):
            cp, inc, qs, lc = u_in[j][r]
            if r == 0:

                @pl.when(self_in)
                def _():
                    lc.wait()

                @pl.when(jnp.logical_not(self_in))
                def _():
                    inc.wait_recv()
            else:
                inc.wait_recv()
            xw[j].append(unit_on(j, b, qs, ng + r, at(1 - b, q, y, c), (1 - b, qs)))
        for r in range(ng):
            qs = u_in[j][r][2]
            qo = lax.rem(g - r + ng, ng) * 2 + 1 - c
            d_in.append(unit_on(j, b, qs, 2 * ng + r, at(b, q, y, 1 - c), (b, qo)))

    def c_round(j):
        for r in range(ng):
            qs = u_in[j][r][2]
            qo = lax.rem(g - r + ng, ng) * 2 + 1 - c
            xw[j][r].wait_recv()
            d_in.append(unit_on(j, 1 - b, qs, 3 * ng + r, at(b, q, y, 1 - c), (1 - b, qo)))

    x_round(0)
    x_round(1)
    c_round(0)
    x_round(2)
    c_round(1)
    c_round(2)
    for cp in c_in + d_in:
        cp.wait_recv()
    for cp in sent:
        cp.wait_send()
    for j in range(len(units)):
        for r in range(ng):
            cp = u_in[j][r][0]
            if r == 0:

                @pl.when(jnp.logical_not(self_in))
                def _():
                    cp.wait_send()
            else:
                cp.wait_send()


def gather_all(nz, qkv, wo, gain, wg, wu, wd):
    ng = nz // 2
    out = [
        jax.ShapeDtypeStruct((2, nz, qkv.shape[0], 4 * qkv.shape[1]), BF16),
        jax.ShapeDtypeStruct((2, nz, 2, 2) + wo.shape, BF16),
        jax.ShapeDtypeStruct((2, nz, 2, 2) + gain.shape, BF16),
        jax.ShapeDtypeStruct((2, nz) + wg.shape, BF16),
        jax.ShapeDtypeStruct((2, nz) + wu.shape, BF16),
        jax.ShapeDtypeStruct((2, nz) + wd.shape, BF16),
    ]
    ns = 2 * nz + 4
    return pl.pallas_call(
        functools.partial(gather_kernel, nz),
        out_shape=out,
        in_specs=[ANY] * 6,
        out_specs=[ANY] * 6,
        scratch_shapes=[
            pltpu.SemaphoreType.DMA((3,)),
            pltpu.SemaphoreType.DMA((3, ns)),
            pltpu.SemaphoreType.DMA((3, ns)),
            pltpu.SemaphoreType.DMA((3,)),
            pltpu.SemaphoreType.DMA((3, 4 * ng)),
            pltpu.SemaphoreType.DMA((3, 4 * ng)),
        ],
        compiler_params=pltpu.CompilerParams(collective_id=0, has_side_effects=True),
    )(qkv, wo, gain, wg, wu, wd)


def reduce_kernel(nz, qkv, wo, gain, wg, wu, wd, qkv_o, wo_o, gain_o, wg_o, wu_o, wd_o, *scratch):
    b, q, y, c = place()
    g, e = q // 2, q % 2
    ng = nz // 2
    qw = qkv_o.shape[1]
    self_in = e == c
    n_items, n_units = 3, 3
    own = scratch[0:3]
    r1 = scratch[3:6]
    r2 = scratch[6:9]
    r3 = scratch[9:12]
    r4 = scratch[12:15]
    uown = scratch[15:18]
    u1 = scratch[18:21]
    u2 = scratch[21:24]
    u3 = scratch[24:27]
    lsem, ssem, rsem, wls, wss, wrs = scratch[27:]
    bar = greet(
        [at(b, lax.rem(q + r, nz), y, c) for r in range(1, nz)]
        + [at(1 - b, q, y, c), at(b, q, 1 - y, c), at(b, q, y, 1 - c)]
        + [at(b, lax.rem(g + r, ng) * 2 + c, y, e) for r in range(1, ng)]
    )
    first = at(b, g * 2 + c, y, e)

    @pl.when(jnp.logical_not(self_in))
    def _():
        pl.semaphore_signal(bar, inc=1, device_id=first, device_id_type=MESH)

    pl.semaphore_wait(bar, nz + 1 + ng - jnp.where(self_in, 1, 0) + 1)

    other_core = at(b, q, y, 1 - c)
    other_y = at(b, q, 1 - y, c)
    other_x = at(1 - b, q, y, c)
    full = (pl.ds(0, 2), pl.ds(0, nz))

    def view_qkv(ref, yy, cc):
        return ref.at[full[0], full[1], :, pl.ds(pl.multiple_of((yy * 2 + cc) * qw, 128), qw)]

    def view_lead(ref, yy, cc):
        return ref.at[full[0], full[1], yy, cc]

    items = [(qkv, qkv_o, view_qkv), (wo, wo_o, view_lead), (gain, gain_o, view_lead)]
    units = [(wd, wd_o), (wg, wg_o), (wu, wu_o)]
    sent = []
    item_local, item_in = [[] for _ in items], [[] for _ in items]
    unit_local, unit_in = [[] for _ in units], [[] for _ in units]

    def start(cp):
        cp.start()
        sent.append(cp)
        return cp

    def item_core(i):
        src, _, view = items[i]
        for yy in range(2):
            item_in[i].append(start(remote(view(src, yy, 1 - c), r1[i].at[yy], ssem.at[i, yy], rsem.at[i, yy], other_core)))
            cp = pltpu.make_async_copy(view(src, yy, c), own[i].at[yy], lsem.at[i, yy])
            cp.start()
            item_local[i].append(cp)

    def unit_core(j):
        src, _ = units[j]
        for xx in range(2):
            for r in range(ng):
                s = xx * ng + r
                mine, yours = r * 2 + c, r * 2 + 1 - c
                unit_in[j].append(start(remote(src.at[xx, yours], u1[j].at[xx, r], wss.at[j, s], wrs.at[j, s], other_core)))
                cp = pltpu.make_async_copy(src.at[xx, mine], uown[j].at[xx, r], wls.at[j, s])
                cp.start()
                unit_local[j].append(cp)

    def add(dst, src, lead):
        def one(n, _):
            dst[n] = (dst[n].astype(F32) + src[n].astype(F32)).astype(dst.dtype)
            return 0

        lax.fori_loop(0, lead, one, 0)

    def unit_x(j):
        for cp in unit_local[j]:
            cp.wait()
        for cp in unit_in[j]:
            cp.wait_recv()
        add(uown[j].at[1 - b], u1[j].at[1 - b], ng)
        cp = start(remote(uown[j].at[1 - b], u2[j], wss.at[j, 2 * ng], wrs.at[j, 2 * ng], other_x))
        add(uown[j].at[b], u1[j].at[b], ng)
        unit_in[j] = [cp]

    def unit_z(j):
        unit_in[j][0].wait_recv()
        add(uown[j].at[b], u2[j], ng)
        waits = []
        for r in range(ng):
            gs = lax.rem(g + r, ng)
            cp = remote(uown[j].at[b, gs], u3[j].at[r], wss.at[j, 2 * ng + 1 + r], wrs.at[j, 2 * ng + 1 + r], at(b, gs * 2 + c, y, e))
            if r == 0:
                lc = pltpu.make_async_copy(uown[j].at[b, gs], u3[j].at[0], wls.at[j, 2 * ng])

                @pl.when(self_in)
                def _():
                    lc.start()

                @pl.when(jnp.logical_not(self_in))
                def _():
                    cp.start()

                waits.append((cp, lc))
            else:
                start(cp)
                waits.append((cp, None))
        unit_in[j] = waits

    def unit_end(j):
        for cp, lc in unit_in[j]:
            if lc is not None:

                @pl.when(self_in)
                def _():
                    lc.wait()

                @pl.when(jnp.logical_not(self_in))
                def _():
                    cp.wait()
            else:
                cp.wait_recv()
        rows = u3[j].shape[1]
        step = 16

        def one(n, _):
            sl = pl.ds(pl.multiple_of(n * step, step), step)
            total = u3[j][0, sl].astype(F32)
            for r in range(1, ng):
                total = total + u3[j][r, sl].astype(F32)
            units[j][1][sl] = total.astype(units[j][1].dtype)
            return 0

        lax.fori_loop(0, rows // step, one, 0)

    def item_y(i):
        for cp in item_local[i]:
            cp.wait()
        for cp in item_in[i]:
            cp.wait_recv()
        for xx in range(2):
            add(own[i].at[1 - y, xx], r1[i].at[1 - y, xx], nz)
        cp = start(remote(own[i].at[1 - y], r2[i], ssem.at[i, 2], rsem.at[i, 2], other_y))
        for xx in range(2):
            add(own[i].at[y, xx], r1[i].at[y, xx], nz)
        item_in[i] = [cp]

    def item_x(i):
        item_in[i][0].wait_recv()
        add(own[i].at[y, 1 - b], r2[i].at[1 - b], nz)
        cp = start(remote(own[i].at[y, 1 - b], r3[i], ssem.at[i, 3], rsem.at[i, 3], other_x))
        add(own[i].at[y, b], r2[i].at[b], nz)
        item_in[i] = [cp]

    def item_z(i):
        item_in[i][0].wait_recv()
        add(own[i].at[y, b], r3[i], nz)
        waits = []
        for r in range(1, nz):
            qt = lax.rem(q + r, nz)
            waits.append(start(remote(own[i].at[y, b, qt], r4[i].at[r - 1], ssem.at[i, 3 + r], rsem.at[i, 3 + r], at(b, qt, y, c))))
        item_in[i] = waits

    def item_end(i):
        for cp in item_in[i]:
            cp.wait_recv()
        total = own[i][y, b, q].astype(F32)
        for r in range(1, nz):
            total = total + r4[i][r - 1].astype(F32)
        items[i][1][...] = total.astype(items[i][1].dtype)

    for j in range(n_units):
        unit_core(j)
    for i in range(n_items):
        item_core(i)
    for j in range(n_units):
        unit_x(j)
    for i in range(n_items):
        item_y(i)
    unit_z(0)
    for i in range(n_items):
        item_x(i)
    unit_z(1)
    for i in range(n_items):
        item_z(i)
    unit_z(2)
    for i in range(n_items):
        item_end(i)
    for j in range(n_units):
        unit_end(j)
    for cp in sent:
        cp.wait_send()


def reduce_all(nz, qkv, wo, gain, wg, wu, wd):
    ng = nz // 2
    qw = qkv.shape[3] // 4
    blocks = [((qkv.shape[2], qw), BF16), (wo.shape[4:], BF16), (gain.shape[4:], F32)]
    ublocks = [(wd.shape[2:], BF16), (wg.shape[2:], BF16), (wu.shape[2:], BF16)]
    scratch = (
        [pltpu.VMEM((2, 2, nz) + s, t) for s, t in blocks]
        + [pltpu.VMEM((2, 2, nz) + s, t) for s, t in blocks]
        + [pltpu.VMEM((2, nz) + s, t) for s, t in blocks]
        + [pltpu.VMEM((nz,) + s, t) for s, t in blocks]
        + [pltpu.VMEM((nz - 1,) + s, t) for s, t in blocks]
        + [pltpu.VMEM((2, ng) + s, t) for s, t in ublocks]
        + [pltpu.VMEM((2, ng) + s, t) for s, t in ublocks]
        + [pltpu.VMEM((ng,) + s, t) for s, t in ublocks]
        + [pltpu.VMEM((ng,) + s, t) for s, t in ublocks]
        + [
            pltpu.SemaphoreType.DMA((3, 2)),
            pltpu.SemaphoreType.DMA((3, nz + 3)),
            pltpu.SemaphoreType.DMA((3, nz + 3)),
            pltpu.SemaphoreType.DMA((3, 2 * ng + 1)),
            pltpu.SemaphoreType.DMA((3, 3 * ng + 1)),
            pltpu.SemaphoreType.DMA((3, 3 * ng + 1)),
        ]
    )
    out = [
        jax.ShapeDtypeStruct(blocks[0][0], BF16),
        jax.ShapeDtypeStruct(blocks[1][0], F32),
        jax.ShapeDtypeStruct(blocks[2][0], F32),
        jax.ShapeDtypeStruct(ublocks[1][0], BF16),
        jax.ShapeDtypeStruct(ublocks[2][0], BF16),
        jax.ShapeDtypeStruct(ublocks[0][0], F32),
    ]
    return pl.pallas_call(
        functools.partial(reduce_kernel, nz),
        out_shape=out,
        in_specs=[ANY] * 6,
        out_specs=[VMEM] * 6,
        scratch_shapes=scratch,
        compiler_params=pltpu.CompilerParams(collective_id=1, has_side_effects=True, vmem_limit_bytes=60 * 2**20),
    )(qkv, wo, gain, wg, wu, wd)


def chunk_scores(q, kk, segq, segk, qidx, j, scale):
    s = lax.dot_general(q, kk, (((1,), (1,)), ((), ())), preferred_element_type=F32) * scale
    kidx = j * 256 + lax.broadcasted_iota(jnp.int32, (1, 256), 1)
    return s, (segq == segk) & (kidx <= qidx)


def attn_fwd_kernel(nb, q_ref, kv_ref, segq_ref, segk_ref, o_ref, lse_ref, kvall, lsem, ssem, rsem):
    b, q, y, c = place()
    k = lax.axis_index("blk")
    nz = nb // 4
    hz = nz // 2
    half = q // hz
    ql = q - half * hz
    low = k < nb // 2
    is_mid = k == nb // 2
    mid = (b, nb // 2)
    bar = greet(
        [at(b, half * hz + lax.rem(ql + r, hz), y, c) for r in range(1, hz)] + [at(b, q, 1 - y, c), at(b, q, y, 1 - c)]
    )

    @pl.when(low)
    def _():
        pl.semaphore_signal(bar, inc=1, device_id=mid, device_id_type=MESH)

    @pl.when(is_mid)
    def _():
        for j in range(nb // 2):
            pl.semaphore_signal(bar, inc=1, device_id=(b, j), device_id_type=MESH)

    pl.semaphore_wait(bar, hz + 1 + jnp.where(low, 1, 0) + jnp.where(is_mid, nb // 2, 0))

    def view(qq, yy, cc):
        return kvall.at[qq, yy, cc]

    sent = []

    def start(cp):
        cp.start()
        sent.append(cp)
        return cp

    mine = pltpu.make_async_copy(kv_ref, view(q, y, c), lsem)
    mine.start()
    other_y = at(b, q, 1 - y, c)
    other_c = at(b, q, y, 1 - c)
    z_in = []
    for r in range(1, hz):
        target = at(b, half * hz + lax.rem(ql + r, hz), y, c)
        start(remote(kv_ref, view(q, y, c), ssem.at[r], rsem.at[r], target))
        src = half * hz + lax.rem(ql - r + hz, hz)
        z_in.append((remote(kv_ref, view(src, y, c), ssem.at[r], rsem.at[r], target), src))
    start(remote(kv_ref, view(q, y, c), ssem.at[hz], rsem.at[hz], other_y))
    y_in = [(remote(kv_ref, view(q, 1 - y, c), ssem.at[hz], rsem.at[hz], other_y), q)]
    ns = 2 * hz + hz * 2
    to_mid = remote(kv_ref, view(q, y, c), ssem.at[ns], rsem.at[ns + k % (nb // 2)], mid)

    @pl.when(low)
    def _():
        to_mid.start()

    mine.wait()
    c_in = []
    s = 2 * hz

    def to_core(qq, yy, s):
        start(remote(view(qq, yy, c), view(qq, yy, c), ssem.at[s], rsem.at[s], other_c))
        c_in.append(remote(view(qq, yy, c), view(qq, yy, 1 - c), ssem.at[s], rsem.at[s], other_c))

    to_core(q, y, s)
    s += 1
    for r, (cp, src) in enumerate(z_in):
        cp.wait_recv()
        n = hz + 1 + r
        start(remote(view(src, y, c), view(src, y, c), ssem.at[n], rsem.at[n], other_y))
        y_in.append((remote(view(src, y, c), view(src, 1 - y, c), ssem.at[n], rsem.at[n], other_y), src))
        to_core(src, y, s)
        s += 1
    for cp, src in y_in:
        cp.wait_recv()
        to_core(src, 1 - y, s)
        s += 1
    for cp in c_in:
        cp.wait_recv()

    @pl.when(is_mid)
    def _():
        for j in range(nb // 2):
            remote(kv_ref, view(j // 4, (j // 2) % 2, j % 2), ssem.at[ns], rsem.at[ns + j], mid).wait_recv()

    scale = HD ** (-0.5)
    lo = jnp.where(k <= nb // 2, 0, nb // 4)
    hi = k // 2 + 1
    rows = q_ref.shape[1]
    tok = rows // H
    qidx = k * tok + lax.broadcasted_iota(jnp.int32, (rows, 1), 0) % tok
    for m in range(q_ref.shape[0]):
        qm = q_ref[m]
        segq = segq_ref[m]

        def body(j, carry):
            mx, sm, acc = carry
            blk = kvall[j // 2, j % 2, :, m].reshape(256, 2 * HD)
            s, ok = chunk_scores(qm, blk[:, :HD], segq, segk_ref[m, j], qidx, j, scale)
            s = jnp.where(ok, s, -1e30)
            new = jnp.maximum(mx, jnp.max(s, axis=-1, keepdims=True))
            p = jnp.where(ok, jnp.exp(s - new), 0.0)
            alpha = jnp.exp(mx - new)
            sm = sm * alpha + jnp.sum(p, axis=-1, keepdims=True)
            acc = acc * alpha + jnp.dot(p.astype(BF16), blk[:, HD:], preferred_element_type=F32)
            return new, sm, acc

        mx, sm, acc = lax.fori_loop(
            lo, hi, body, (jnp.full((rows, 1), -1e30, F32), jnp.zeros((rows, 1), F32), jnp.zeros((rows, HD), F32))
        )
        o_ref[m] = acc / sm
        lse_ref[m] = mx + jnp.log(sm)
    for cp in sent:
        cp.wait_send()

    @pl.when(low)
    def _():
        to_mid.wait_send()


def attn_fwd(nb, q, kv, segq, segk):
    nz = nb // 4
    ns = 4 * (nz // 2)
    return pl.pallas_call(
        functools.partial(attn_fwd_kernel, nb),
        out_shape=[
            jax.ShapeDtypeStruct(q.shape, F32),
            jax.ShapeDtypeStruct(q.shape[:2] + (1,), F32),
            jax.ShapeDtypeStruct((nz, 2, 2) + kv.shape, BF16),
        ],
        in_specs=[VMEM] * 4,
        out_specs=[VMEM] * 3,
        scratch_shapes=[
            pltpu.SemaphoreType.DMA,
            pltpu.SemaphoreType.DMA((ns + 1,)),
            pltpu.SemaphoreType.DMA((ns + nb // 2,)),
        ],
        compiler_params=pltpu.CompilerParams(collective_id=2, has_side_effects=True, vmem_limit_bytes=60 * 2**20),
    )(q, kv, segq, segk)


def attn_bwd_kernel(
    nb, q_ref, kvall, do_ref, lse_ref, delta_ref, segq_ref, segk_ref, dq_ref, dkv_ref, part, r1, r2, r3, r4, ssem, rsem, msem, nsem
):
    b, q, y, c = place()
    k = lax.axis_index("blk")
    nz = nb // 4
    hz = nz // 2
    half = q // hz
    ql = q - half * hz
    low = k < nb // 2
    is_mid = k == nb // 2
    mid = (b, nb // 2)
    bar = greet(
        [at(b, half * hz + lax.rem(ql + r, hz), y, c) for r in range(1, hz)] + [at(b, q, 1 - y, c), at(b, q, y, 1 - c)]
    )

    @pl.when(low)
    def _():
        pl.semaphore_signal(bar, inc=1, device_id=mid, device_id_type=MESH)

    @pl.when(is_mid)
    def _():
        for j in range(nb // 2):
            pl.semaphore_signal(bar, inc=1, device_id=(b, j), device_id_type=MESH)

    pl.semaphore_wait(bar, hz + 1 + jnp.where(low, 1, 0) + jnp.where(is_mid, nb // 2, 0))
    other_y = at(b, q, 1 - y, c)
    other_c = at(b, q, y, 1 - c)
    sent = []

    def start(cp):
        cp.start()
        sent.append(cp)
        return cp

    def clear(n, _):
        part[half * hz + n // 4, (n // 2) % 2, n % 2] = jnp.zeros(part.shape[3:], BF16)
        return 0

    lax.fori_loop(0, 4 * hz, clear, 0)
    scale = HD ** (-0.5)
    lo = jnp.where(k <= nb // 2, 0, nb // 4)
    hi = k // 2 + 1
    rows = q_ref.shape[1]
    tok = rows // H
    qidx = k * tok + lax.broadcasted_iota(jnp.int32, (rows, 1), 0) % tok
    tn = (((0,), (0,)), ((), ()))
    nt = (((1,), (1,)), ((), ()))
    for m in range(q_ref.shape[0]):
        dq_ref[m] = jnp.zeros(dq_ref.shape[1:], F32)

        def body(j, _):
            qm, dom = q_ref[m], do_ref[m]
            blk = kvall[j // 2, j % 2, :, m].reshape(256, 2 * HD)
            s, ok = chunk_scores(qm, blk[:, :HD], segq_ref[m], segk_ref[m, j], qidx, j, scale)
            p = jnp.where(ok, jnp.exp(jnp.where(ok, s, -1e30) - lse_ref[m]), 0.0)
            dp = lax.dot_general(dom, blk[:, HD:], nt, preferred_element_type=F32)
            ds = (p * (dp - delta_ref[m])).astype(BF16)
            dq_ref[m] += jnp.dot(ds, blk[:, :HD], preferred_element_type=F32) * scale
            dk = lax.dot_general(ds, qm, tn, preferred_element_type=F32) * scale
            dv = lax.dot_general(p.astype(BF16), dom, tn, preferred_element_type=F32)
            part[j // 2, j % 2, :, m] = jnp.concatenate([dk, dv], axis=1).astype(BF16).reshape(2, tok, 2 * HD)
            return 0

        lax.fori_loop(lo, hi, body, 0)

    @pl.when(is_mid)
    def _():
        for j in range(nb // 2):
            remote(part.at[j // 4, (j // 2) % 2, j % 2], r4, msem.at[j], nsem, (b, j)).start()

    hs = pl.ds(half * hz, hz)
    cp = start(remote(part.at[hs, :, 1 - c], r1, ssem.at[0], rsem.at[0], other_c))
    cp.wait_recv()

    def add1(n, _):
        i = half * hz + n // 2
        part[i, n % 2, c] = (part[i, n % 2, c].astype(F32) + r1[n // 2, n % 2].astype(F32)).astype(BF16)
        return 0

    lax.fori_loop(0, 2 * hz, add1, 0)
    cp = start(remote(part.at[hs, 1 - y, c], r2, ssem.at[1], rsem.at[1], other_y))
    cp.wait_recv()

    def add2(n, _):
        i = half * hz + n
        part[i, y, c] = (part[i, y, c].astype(F32) + r2[n].astype(F32)).astype(BF16)
        return 0

    lax.fori_loop(0, hz, add2, 0)
    last = []
    for r in range(1, hz):
        qt = half * hz + lax.rem(ql + r, hz)
        last.append(start(remote(part.at[qt, y, c], r3.at[r - 1], ssem.at[1 + r], rsem.at[1 + r], at(b, qt, y, c))))
    total = part[q, y, c].astype(F32)
    for r, cp in enumerate(last):
        cp.wait_recv()
        total = total + r3[r].astype(F32)
    dkv_ref[...] = total

    @pl.when(low)
    def _():
        remote(part.at[0, 0, 0], r4, msem.at[0], nsem, mid).wait_recv()
        dkv_ref[...] += r4[...].astype(F32)

    for cp in sent:
        cp.wait_send()

    @pl.when(is_mid)
    def _():
        for j in range(nb // 2):
            remote(part.at[j // 4, (j // 2) % 2, j % 2], r4, msem.at[j], nsem, (b, j)).wait_send()


def attn_bwd(nb, q, kvall, do, lse, delta, segq, segk):
    nz = nb // 4
    hz = nz // 2
    blk = kvall.shape[3:]
    return pl.pallas_call(
        functools.partial(attn_bwd_kernel, nb),
        out_shape=[jax.ShapeDtypeStruct(q.shape, F32), jax.ShapeDtypeStruct(blk, F32)],
        in_specs=[VMEM] * 7,
        out_specs=[VMEM] * 2,
        scratch_shapes=[
            pltpu.VMEM(kvall.shape, BF16),
            pltpu.VMEM((hz, 2) + blk, BF16),
            pltpu.VMEM((hz,) + blk, BF16),
            pltpu.VMEM((hz - 1,) + blk, BF16),
            pltpu.VMEM(blk, BF16),
            pltpu.SemaphoreType.DMA((hz + 1,)),
            pltpu.SemaphoreType.DMA((hz + 1,)),
            pltpu.SemaphoreType.DMA((nb // 2,)),
            pltpu.SemaphoreType.DMA,
        ],
        compiler_params=pltpu.CompilerParams(collective_id=3, has_side_effects=True, vmem_limit_bytes=60 * 2**20),
    )(q, kvall, do, lse, delta, segq, segk)


def tiles(n, w):
    return [(i, min(w, n - i)) for i in range(0, n, w)]


def gelu_parts(z):
    k0 = math.sqrt(2.0 / math.pi)
    t = jnp.tanh(k0 * (z + 0.044715 * z * z * z))
    value = 0.5 * z * (1.0 + t)
    slope = 0.5 * (1.0 + t) + 0.5 * z * (1.0 - t * t) * (k0 * (1.0 + 3.0 * 0.044715 * z * z))
    return value, slope


def ffn_kernel(
    b_ref, h1_ref, dy_ref, gp_ref, wg, wu, wd, out_ref, db_ref, dgp_ref, gg_o, gu_o, gd_o,
    ball, ballt, gate, up, mm, fsend, frecv, dfall, dsend, drecv, sg, su, sd, ssem, rsem, osem,
):
    b, q, y, c = place()
    g = q // 2
    t = lax.rem(q, 2) * 2 + y
    micro, tok, width = b_ref.shape
    hidden = wd.shape[0]
    peers = []
    for p in range(1, 4):
        tt = lax.rem(t + p, 4)
        peers.append((p, tt, at(b, g * 2 + tt // 2, lax.rem(tt, 2), c)))
    bar = greet([p[2] for p in peers])
    pl.semaphore_wait(bar, 3)
    sent = []
    nt = (((1,), (1,)), ((), ()))

    def spread(phase, m, src, dst_of, recv_of):
        waits = []
        for p, tt, target in peers:
            cp = remote(src(tt), dst_of(p, tt), ssem.at[phase, m, p - 1], rsem.at[phase, m, p - 1], target)
            cp.start()
            sent.append(cp)
            ts = lax.rem(t + 4 - p, 4)
            waits.append(remote(src(tt), recv_of(p, ts), ssem.at[phase, m, p - 1], rsem.at[phase, m, p - 1], target))
        return waits

    a_in, f_in, df_in, db_in = [], [], [], []
    for m in range(micro):
        a_in.append(
            spread(0, m, lambda tt, m=m: b_ref.at[m], lambda p, tt, m=m: ball.at[m, t], lambda p, ts, m=m: ball.at[m, ts])
        )
        ball[m, t] = b_ref[m]

    def forward(m):
        for cp in a_in[m]:
            cp.wait_recv()

        def body(n, _):
            cols = pl.ds(pl.multiple_of(n * 256, 256), 256)
            x = ball[m].reshape(4 * tok, width)
            gv = jnp.dot(x, wg[:, cols], preferred_element_type=F32)
            uv = jnp.dot(x, wu[:, cols], preferred_element_type=F32)
            gate[m, :, cols] = gv.astype(BF16)
            up[m, :, cols] = uv.astype(BF16)
            mm[m, :, cols] = (gelu_parts(gv)[0] * uv).astype(BF16)
            return 0

        lax.fori_loop(0, hidden // 256, body, 0)
        for o, w in tiles(width, 256):
            f = jnp.dot(mm[m], wd[:, o : o + w], preferred_element_type=F32)
            fsend[m, :, :, o : o + w] = f.astype(BF16).reshape(4, tok, w)
        f_in.append(
            spread(1, m, lambda tt: fsend.at[m, tt], lambda p, tt: frecv.at[m, p - 1], lambda p, ts: frecv.at[m, p - 1])
        )

    def middle(m):
        for cp in f_in[m]:
            cp.wait_recv()
        f = fsend[m, t].astype(F32)
        for p in range(3):
            f = f + frecv[m, p].astype(F32)
        gp = 1.0 + gp_ref[...]
        r = lax.rsqrt(jnp.mean(f * f, axis=-1, keepdims=True) + epsilon)
        n = f * r
        dy = dy_ref[m].astype(F32)
        out_ref[m] = (h1_ref[m] + n * gp).astype(BF16)
        dg = dy * gp
        df = r * (dg - n * jnp.mean(dg * n, axis=-1, keepdims=True))
        part = jnp.sum(dy * n, axis=0, keepdims=True)
        if m == 0:
            dgp_ref[...] = part
        else:
            dgp_ref[...] += part
        dfall[m, t] = df.astype(BF16)
        df_in.append(
            spread(2, m, lambda tt: dfall.at[m, t], lambda p, tt: dfall.at[m, t], lambda p, ts: dfall.at[m, ts])
        )

    def backward(m):
        for cp in df_in[m]:
            cp.wait_recv()

        def body(n, _):
            cols = pl.ds(pl.multiple_of(n * 256, 256), 256)
            x = dfall[m].reshape(4 * tok, width)
            dm = lax.dot_general(x, wd[cols, :], nt, preferred_element_type=F32)
            value, slope = gelu_parts(gate[m, :, cols].astype(F32))
            uv = up[m, :, cols].astype(F32)
            gate[m, :, cols] = (dm * uv * slope).astype(BF16)
            up[m, :, cols] = (dm * value).astype(BF16)
            return 0

        lax.fori_loop(0, hidden // 256, body, 0)
        for o, w in tiles(width, 256):
            d = lax.dot_general(gate[m], wg[o : o + w, :], nt, preferred_element_type=F32)
            d = d + lax.dot_general(up[m], wu[o : o + w, :], nt, preferred_element_type=F32)
            dsend[m, :, :, o : o + w] = d.astype(BF16).reshape(4, tok, w)
        db_in.append(
            spread(3, m, lambda tt: dsend.at[m, tt], lambda p, tt: drecv.at[m, p - 1], lambda p, ts: drecv.at[m, p - 1])
        )

    for m in range(micro):
        forward(m)
    for m in range(micro):
        for i in range(4):
            ballt[:, (m * 4 + i) * tok : (m * 4 + i + 1) * tok] = ball[m, i].T
    for m in range(micro):
        middle(m)
    for m in range(micro):
        backward(m)

    def grads(n, _):
        cols = pl.ds(pl.multiple_of(n * 256, 256), 256)
        slot = lax.rem(n, 2)

        def out(m, o):
            cc = pl.ds(pl.multiple_of(m * 256, 256), 256)
            return [
                pltpu.make_async_copy(sg.at[o], gg_o.at[:, cc], osem.at[0, o]),
                pltpu.make_async_copy(su.at[o], gu_o.at[:, cc], osem.at[1, o]),
                pltpu.make_async_copy(sd.at[o], gd_o.at[cc, :], osem.at[2, o]),
            ]

        @pl.when(n >= 2)
        def _():
            for cp in out(n, slot):
                cp.wait()

        x = ballt[...]
        sg[slot] = jnp.dot(x, gate[:, :, cols].reshape(-1, 256), preferred_element_type=F32).astype(BF16)
        su[slot] = jnp.dot(x, up[:, :, cols].reshape(-1, 256), preferred_element_type=F32).astype(BF16)
        sd[slot] = jnp.dot(
            mm[:, :, cols].reshape(-1, 256).T, dfall[...].reshape(-1, width), preferred_element_type=F32
        ).astype(BF16)
        for cp in out(n, slot):
            cp.start()
        return 0

    steps = hidden // 256
    lax.fori_loop(0, steps, grads, 0)
    for n in range(max(steps - 2, 0), steps):
        o = n % 2
        pltpu.make_async_copy(sg.at[o], gg_o.at[:, n * 256 : n * 256 + 256], osem.at[0, o]).wait()
        pltpu.make_async_copy(su.at[o], gu_o.at[:, n * 256 : n * 256 + 256], osem.at[1, o]).wait()
        pltpu.make_async_copy(sd.at[o], gd_o.at[n * 256 : n * 256 + 256, :], osem.at[2, o]).wait()
    for m in range(micro):
        for cp in db_in[m]:
            cp.wait_recv()
        d = dsend[m, t].astype(F32)
        for p in range(3):
            d = d + drecv[m, p].astype(F32)
        db_ref[m] = d
    for cp in sent:
        cp.wait_send()


def ffn(b, h1, dy, gp, wg, wu, wd):
    micro, tok, width = b.shape
    hidden = wd.shape[0]
    wide = (micro, 4 * tok, hidden)
    return pl.pallas_call(
        ffn_kernel,
        out_shape=[
            jax.ShapeDtypeStruct(b.shape, BF16),
            jax.ShapeDtypeStruct(b.shape, F32),
            jax.ShapeDtypeStruct((1, width), F32),
            jax.ShapeDtypeStruct(wg.shape, BF16),
            jax.ShapeDtypeStruct(wu.shape, BF16),
            jax.ShapeDtypeStruct(wd.shape, BF16),
        ],
        in_specs=[VMEM] * 7,
        out_specs=[VMEM] * 3 + [ANY] * 3,
        scratch_shapes=[
            pltpu.VMEM((micro, 4, tok, width), BF16),
            pltpu.VMEM((width, micro * 4 * tok), BF16),
            pltpu.VMEM(wide, BF16),
            pltpu.VMEM(wide, BF16),
            pltpu.VMEM(wide, BF16),
            pltpu.VMEM((micro, 4, tok, width), BF16),
            pltpu.VMEM((micro, 3, tok, width), BF16),
            pltpu.VMEM((micro, 4, tok, width), BF16),
            pltpu.VMEM((micro, 4, tok, width), BF16),
            pltpu.VMEM((micro, 3, tok, width), BF16),
            pltpu.VMEM((2, width, 256), BF16),
            pltpu.VMEM((2, width, 256), BF16),
            pltpu.VMEM((2, 256, width), BF16),
            pltpu.SemaphoreType.DMA((4, micro, 3)),
            pltpu.SemaphoreType.DMA((4, micro, 3)),
            pltpu.SemaphoreType.DMA((3, 2)),
        ],
        compiler_params=pltpu.CompilerParams(collective_id=4, has_side_effects=True, vmem_limit_bytes=62 * 2**20),
    )(b, h1, dy, gp, wg, wu, wd)


def scaled_norm(values, gain):
    return values * lax.rsqrt(jnp.mean(values * values, axis=-1, keepdims=True) + epsilon) * (1.0 + gain)


def segments(lengths, index):
    docs = lengths.shape[1]
    ends = [sum(lengths[:, j] for j in range(i + 1)) for i in range(docs)]
    seg = jnp.zeros((lengths.shape[0], index.shape[0]), jnp.int32)
    first = jnp.zeros_like(seg)
    for i in range(docs):
        past = index[None, :] >= ends[i][:, None]
        seg = seg + past.astype(jnp.int32)
        first = first + jnp.where(past, lengths[:, i][:, None], 0)
    return seg, index[None, :] - first


def rotate(values, cosine, sine):
    half = values.shape[-1] // 2
    a, b = values[..., :half], values[..., half:]
    return jnp.concatenate([a * cosine - b * sine, b * cosine + a * sine], axis=-1)


def middle(attn_value, x_value, gain_attn, gain_pre):
    hidden = x_value + scaled_norm(attn_value, gain_attn)
    return (hidden, scaled_norm(hidden, gain_pre))


def shards(tokens, cotangent, doc_lengths, w_query, w_key, w_value, w_out, w_gate, w_up, w_down, *gains):
    nb = lax.axis_size("blk")
    nz = nb // 4
    me = lax.axis_index("blk")
    _, micro, tok, width = tokens.shape
    n_dev = 2 * nb
    nq = 2 * nz
    kr = w_gate.shape[0]
    qr, qp = 4 * kr, up16(4 * kr)
    dr = w_down.shape[0]
    dp = up16(dr)
    orow = w_out.shape[0]
    op = up16(orow)
    groups = [[4 * i + j for j in range(4)] for i in range(nz)]

    def fit(x, rows):
        return x if x.shape[0] == rows else jnp.pad(x, ((0, rows - x.shape[0]), (0, 0)))

    def slices(w):
        w = jnp.pad(w.reshape(kr, nq, 4, dr), ((0, 0), (0, 0), (0, 0), (0, dp - dr)))
        return w.transpose(2, 0, 1, 3).reshape(4, kr, nq * dp)

    fs = nq * dp
    w_qkv = jnp.concatenate([w_query, w_key, w_value], axis=1)
    qw = w_qkv.shape[1] // 4
    pack = jnp.concatenate([slices(w_gate), slices(w_up), w_qkv.reshape(kr, 4, qw).transpose(1, 0, 2)], axis=2)
    pack = lax.all_to_all(pack, "blk", split_axis=0, concat_axis=0, axis_index_groups=groups, tiled=True)
    pack = fit(pack.reshape(qr, 2 * fs + qw), qp)
    wide = [gain.shape[0] for gain in gains]
    flat = jnp.concatenate(gains)
    flat = jnp.pad(flat, (0, 16 * 128 - flat.shape[0])).reshape(16, 128)

    qkv_f, wo_f, gain_f, wg_f, wu_f, wd_f = gather_all(
        nz, pack[:, 2 * fs :], fit(w_out, op), flat, pack[:, :fs], pack[:, fs : 2 * fs], fit(w_down, dp)
    )
    wqkv = qkv_f[:, :, :qr].reshape(width, 4 * qw)
    wo = wo_f[:, :, :, :, :orow].reshape(n_dev * orow, width)
    wg = wg_f[:, :, :qr].reshape(width, fs)
    wu = wu_f[:, :, :qr].reshape(width, fs)
    wd = wd_f.reshape(fs, width)
    gain_rows = gain_f.reshape(n_dev, 16 * 128)
    full_gains, o = [], 0
    for w in wide:
        full_gains.append(gain_rows[:, o : o + w].reshape(n_dev * w).astype(F32))
        o += w
    gain_in, gain_query, gain_key, gain_attn, gain_pre, gain_post = full_gains

    lengths = doc_lengths[0]
    seg_all, pos_all = segments(lengths, jnp.arange(nb * tok, dtype=jnp.int32))
    seg_me, pos = segments(lengths, me * tok + jnp.arange(tok, dtype=jnp.int32))
    segq = jnp.tile(seg_me, (1, H))[:, :, None]
    segk = seg_all.reshape(micro, nb * tok // 256, 1, 256)
    freq = 1000000.0 ** (-(jnp.arange(HD // 2, dtype=F32) * 2.0 / HD))
    angle = pos.reshape(micro * tok).astype(F32)[:, None] * freq[None, :]
    cosine, sine = jnp.cos(angle), jnp.sin(angle)

    rows = micro * tok
    x = tokens[0].reshape(rows, width).astype(F32)
    dy = cotangent[0].reshape(rows, width)
    normed, pre_pull = jax.vjp(scaled_norm, x, gain_in)
    a = normed.astype(BF16)
    qkv = jnp.dot(a, wqkv, preferred_element_type=F32)
    n_q = H * HD
    q_raw = qkv[:, :n_q].reshape(rows, H, HD)
    k_raw = qkv[:, n_q : n_q + HD]
    v = qkv[:, n_q + HD :].astype(BF16)
    queries, query_pull = jax.vjp(
        lambda r, g: rotate(scaled_norm(r, g), cosine[:, None], sine[:, None]), q_raw, gain_query
    )
    keys, key_pull = jax.vjp(lambda r, g: rotate(scaled_norm(r, g), cosine, sine), k_raw, gain_key)

    def by_head(z):
        return z.reshape(micro, tok, H, HD).transpose(0, 2, 1, 3).reshape(micro, H * tok, HD)

    def by_row(z):
        return z.reshape(micro, H, tok, HD).transpose(0, 2, 1, 3).reshape(rows, H * HD)

    qh = by_head(queries.astype(BF16))
    kv = jnp.concatenate([keys.astype(BF16), v], axis=1).reshape(micro, tok, 2 * HD)
    oh, lse, kvall = attn_fwd(nb, qh, kv, segq, segk)
    o_b = by_row(oh.astype(BF16))
    attn = jnp.dot(o_b, wo, preferred_element_type=F32)
    (h1, ffn_in), mid_pull = jax.vjp(middle, attn, x, gain_attn, gain_pre)

    shape = (micro, tok, width)
    out, db, dg_post, gg, gu, gd = ffn(
        ffn_in.astype(BF16).reshape(shape), h1.reshape(shape), dy.reshape(shape), gain_post[None, :], wg, wu, wd
    )
    d_attn, d_x_mid, dg_attn, dg_pre = mid_pull((dy.astype(F32), db.reshape(rows, width)))
    d_attn = d_attn.astype(BF16)
    grad_out = lax.dot_general(o_b, d_attn, (((0,), (0,)), ((), ())), preferred_element_type=F32).astype(BF16)
    do = lax.dot_general(d_attn, wo, (((1,), (1,)), ((), ())), preferred_element_type=F32).astype(BF16)
    doh = by_head(do)
    delta = jnp.sum(doh.astype(F32) * oh, axis=-1, keepdims=True)
    dqh, dkv = attn_bwd(nb, qh, kvall, doh, lse, delta, segq, segk)
    dkv = dkv.reshape(rows, 2 * HD)
    dq_raw, dg_query = query_pull(by_row(dqh).reshape(rows, H, HD))
    dk_raw, dg_key = key_pull(dkv[:, :HD])
    d_qkv = jnp.concatenate([dq_raw.reshape(rows, n_q), dk_raw, dkv[:, HD:]], axis=1).astype(BF16)
    grad_qkv = lax.dot_general(a, d_qkv, (((0,), (0,)), ((), ())), preferred_element_type=F32).astype(BF16)
    da = lax.dot_general(d_qkv, wqkv, (((1,), (1,)), ((), ())), preferred_element_type=F32)
    d_x_pre, dg_in = pre_pull(da)
    d_x = (d_x_mid + d_x_pre).astype(BF16)

    def quads(z, r, p):
        z = z.reshape(2, nz, r, z.shape[-1])
        return z if r == p else jnp.pad(z, ((0, 0), (0, 0), (0, p - r), (0, 0)))

    go = grad_out.reshape(2, nz, 2, 2, orow, width)
    if op != orow:
        go = jnp.pad(go, ((0, 0),) * 4 + ((0, op - orow), (0, 0)))
    dgains = jnp.concatenate(
        [d.reshape(n_dev, w) for d, w in zip((dg_in, dg_query, dg_key, dg_attn, dg_pre, dg_post[0]), wide)], axis=1
    )
    used = dgains.shape[1]
    dgains = jnp.pad(dgains, ((0, 0), (0, 8 * 128 - used))).reshape(2, nz, 2, 2, 8, 128)
    s_qkv, s_wo, s_gain, s_wg, s_wu, s_wd = reduce_all(
        nz, quads(grad_qkv, qr, qp), go, dgains, quads(gg, qr, qp), quads(gu, qr, qp), gd.reshape(2, nz, dp, width)
    )
    back = jnp.concatenate([s_wg, s_wu, s_qkv], axis=1)[:qr].reshape(4, kr, 2 * fs + qw)
    back = lax.all_to_all(back, "blk", split_axis=0, concat_axis=0, axis_index_groups=groups, tiled=True)
    back = back.astype(F32)

    def rows_of(z):
        z = z.reshape(4, kr, nq, dp)[..., :dr]
        return z.transpose(1, 2, 0, 3).reshape(kr, nq * 4 * dr)

    s_qkv = back[:, :, 2 * fs :].transpose(1, 0, 2).reshape(kr, 4 * qw)
    flat = s_gain.reshape(-1)
    gain_grads, o = [], 0
    for w in wide:
        gain_grads.append(flat[o : o + w])
        o += w
    return (
        out[None],
        d_x.reshape(shape)[None],
        s_qkv[:, :n_q],
        s_qkv[:, n_q : n_q + HD],
        s_qkv[:, n_q + HD :],
        s_wo[:orow],
        rows_of(back[:, :, :fs]),
        rows_of(back[:, :, fs : 2 * fs]),
        s_wd[:dr],
        *gain_grads,
    )


def solution(mesh):
    sequence = P("bucket", None, "blk", None)
    split = ("bucket", "blk")
    return jax.shard_map(
        shards,
        mesh=mesh,
        in_specs=(sequence, sequence, P("bucket", None, None)) + (P(split, None),) * 7 + (P(split),) * 6,
        out_specs=(sequence, sequence) + (P(split, None),) * 7 + (P(split),) * 6,
        check_vma=False,
    )
```

time: 2430 us -> 569 us (0.23)
  blocking collectives: 1050 us -> 0 us
  starting transfers between devices: 612 us -> 16.2 us
  Pallas kernels: 0 us -> 430 us
  matrix products: 388 us -> 14.3 us
  local copies, waits for them, and re-layouts: 156 us -> 49.4 us
  other arithmetic: 99.1 us -> 23.3 us
  waiting for transfers between devices: 81.3 us -> 22.9 us
    unnamed x4 -> x0, blocking collectives: 967 us -> none
    ppermute x184 -> x0, starting transfers between devices: 557 us -> none  [the longest x120 485 us: shifted(): return lax.ppermute(block, axis, route)]
    pallas_call x0 -> x5, Pallas kernels: none -> 430 us  [the longest x1 131 us: gather_all(): pl.pallas_call(functools.partial(gather_kernel, nz), out_shape=out, in_sp...]
    dot_general x266 -> x6, matrix products: 388 us -> 14.3 us  [the longest x1 4.13 us: shards(): lax.dot_general(d_qkv, wqkv, (((1,), (1,)), ((), ())), preferred_element_...]
    unnamed x435 -> x84, local copies, waits for them, and re-layouts: 136 us -> 9.01 us
    all_gather x2 -> x0, blocking collectives: 83.1 us -> none  [the longest x1 42.3 us: fetch(): lax.all_gather(w_value, ('bucket', 'blk'), axis=0, tiled=True)]
    ppermute x184 -> x0, waiting for transfers between devices: 55.4 us -> none  [the longest x64 28.7 us: from_behind(): lax.ppermute(x, axis, [(i, (i + by) % devices) for i in range(devices)])]
    unnamed x21 -> x0, starting transfers between devices: 55.1 us -> none
  transfers between devices with their start and end apart: 211 -> 2, of which waited for: 54 -> 2; matrix products, arithmetic and copies ran while one was open for 42% -> 1% of each run, Pallas kernels for 0% -> 0%
where the time goes in v1:
time: 569 us; the launch traced here: 558 us
  Pallas kernels  430 us (76%)
  local copies, waits for them, and re-layouts  49.4 us (9%)
  other arithmetic  23.3 us (4%)
  waiting for transfers between devices  22.9 us (4%)
  starting transfers between devices  16.2 us (3%)
  matrix products  14.3 us (3%)
    pallas_call x1, Pallas kernels, gather_all(): pl.pallas_call(functools.partial(gather_kernel, nz), out_shape=out, in_sp...  131 us
    pallas_call x1, Pallas kernels, reduce_all(): pl.pallas_call(functools.partial(reduce_kernel, nz), out_shape=out, in_sp...  122 us
    pallas_call x1, Pallas kernels, ffn(): pl.pallas_call(ffn_kernel, out_shape=[jax.ShapeDtypeStruct(b.shape, BF16)...  115 us
    pallas_call x1, Pallas kernels, attn_bwd(): pl.pallas_call(functools.partial(attn_bwd_kernel, nb), out_shape=[jax.Sha...  35.8 us
    pallas_call x1, Pallas kernels, attn_fwd(): pl.pallas_call(functools.partial(attn_fwd_kernel, nb), out_shape=[jax.Sha...  25.4 us
    all_to_all x1, waiting for transfers between devices, shards(): lax.all_to_all(back, 'blk', split_axis=0, concat_axis=0, axis_index_group...  12.7 us
    all_to_all x1, starting transfers between devices, shards(): lax.all_to_all(back, 'blk', split_axis=0, concat_axis=0, axis_index_group...  11.8 us
  transfers between devices with their start and end apart: 2, of which 2 were waited for; matrix products, arithmetic and copies ran while one was open for 1% of the time, Pallas kernels for 0%

profile of v1, /device:TPU:7, one launch (start us, length us, event | category | flops | bytes accessed | tf_op | source)
XLA Modules:
  0.0 557.8 jit_solution(17656105110441283086)
XLA Ops:
  0.6 2.8 reshape.692
  4.7 1.7 reshape.694
  9.3 4.5 all-to-all-start
  18.6 10.2 %all-to-all-done = bf16[4,36,3968]{2,1,0:T(8,128)(2,1)S(1)} async-done(((bf16[4,36,3968]{2,1,0:T(8,128)(2,1)}), bf16[4,36,3968]{2,1,0:T(8,128)(2,1)S(1)}, u32[]{:S(2)}, u32[]{:S(2)}) %all-to-all-start) | async-done | bytes 1142816 | tf_op jit(solution)/shard_map/all_to_all | solution.py:1038
  30.7 131.3 %shard_map.271 = (bf16[2,4,144,1536]{3,2,1,0:T(8,128)(2,1)}, bf16[2,4,2,2,32,1152]{5,4,3,2,1,0:T(8,128)(2,1)}, bf16[2,4,2,2,16,128]{5,4,3,2,1,0:T(8,128)(2,1)}, ...) custom-call(bf16[144,384]{1,0:T(8,128)(2,1)} %slice.169.qkv, ...), custom_call_target="tpu_custom_call" | custom-call | tf_op jit(solution)/shard_map/pallas_call | solution.py:238
  163.4 3.2 fusion.58
  173.0 25.4 %shard_map.272 = (f32[2,512,256]{2,1,0:T(8,128)}, f32[2,512,1]{2,1,0:T(8,128)}, bf16[4,2,2,2,128,512]{5,4,3,2,1,0:T(8,128)(2,1)}) custom-call(bf16[2,512,256]{2,1,0:T(8,128)(2,1)} %bitcast.200, bf16[2,128,512]{2,1,0:T(8,128)(2,1)} %bitcast.220, s32[2,512,1]{2,1,0:T(8,128)} %tile.10.segq_ref, s32[2,8,1,256]{3,2,1,0:T(1,128)} %fusion.33.segk_ref), custom_call_target="tpu_custom_call" | custom-call | tf_op jit(solution)/shard_map/pallas_call | solution.py:621
  198.4 1.4 convert_element_type.210
  204.3 115.1 %shard_map.273 = (bf16[2,128,1152]{2,1,0:T(8,128)(2,1)}, f32[2,128,1152]{2,1,0:T(8,128)}, f32[1,1152]{1,0:T(1,128)}, bf16[1152,1792]{1,0:T(8,128)(2,1)}, bf16[11...) custom-call(bf16[2,128,1152]{2,1,0:T(8,128)(2,1)} %bitcast.210, f32[2,128,1152]{2,1,0:T(8,128)} %bitcast.191, ...), custom_call_target="tpu_custom_call" | custom-call | tf_op jit(solution)/shard_map/pallas_call | solution.py:951
  319.4 2.1 fusion.3
  321.7 2.2 multiply_reduce_fusion
  330.3 35.8 %shard_map.274 = (f32[2,512,256]{2,1,0:T(8,128)}, f32[2,128,512]{2,1,0:T(8,128)}) custom-call(bf16[2,512,256]{2,1,0:T(8,128)(2,1)} %bitcast.201, bf16[4,2,2,2,128,512]{5,4,3,2,1,0:T(8,128)(2,1)} %get-tuple-element.47.kvall, bf16[2,512,256]{2,1,0:T(8,128)(2,1)} %bitcast.199, f32[2,512,1]{2,1,0:T(8,128)} %get-tuple-element.48.lse_ref, ...), custom_call_target="tpu_custom_call" | custom-call | tf_op jit(solution)/shard_map/pallas_call | solution.py:757
  366.1 1.6 fusion.29
  368.7 2.3 convolution_convert_fusion.1
  377.9 4.1 fusion.7
  388.0 2.0 fusion.6
  390.0 2.9 convolution_convert_fusion
  392.9 122.1 %shard_map.275 = (bf16[144,384]{1,0:T(8,128)(2,1)}, f32[32,1152]{1,0:T(8,128)}, f32[8,128]{1,0:T(8,128)}, bf16[144,1792]{1,0:T(8,128)(2,1)}, bf16[144,1792]{1,0:T(8,128)(2,1)}, /*index=5*/f32[224,1152]{1,0:T(8,128)}) custom-call(bf16[2,4,144,1536]{3,2,1,0:T(8,128)(2,1)} %bitcast.195, bf16[2,4,2,2,32,1152]{5,4,3,2,1,0:T(8,128)(2,1)} %bitcast.196, ...), custom_call_target="tpu_custom_call" | custom-call | tf_op jit(solution)/shard_map/pallas_call | solution.py:484
  515.1 1.3 pad_maximum_fusion.1
  517.6 11.8 %all-to-all-start.1 = ((bf16[4,36,3968]{2,1,0:T(8,128)(2,1)}), bf16[4,36,3968]{2,1,0:T(8,128)(2,1)S(1)}, u32[]{:S(2)}, u32[]{:S(2)}) async-start(bf16[4,36,3968]{2,1,0:T(8,128)(2,1)} %reshape.729), calls=%async_computation.1 | async-start | bytes 2539520 | tf_op jit(solution)/shard_map/all_to_all | solution.py:1132
  531.6 12.7 %all-to-all-done.1 = bf16[4,36,3968]{2,1,0:T(8,128)(2,1)S(1)} async-done(((bf16[4,36,3968]{2,1,0:T(8,128)(2,1)}), bf16[4,36,3968]{2,1,0:T(8,128)(2,1)S(1)}, u32[]{:S(2)}, u32[]{:S(2)}) %all-to-all-start.1) | async-done | bytes 1142816 | tf_op jit(solution)/shard_map/all_to_all | solution.py:1132
  547.1 2.0 reshape.739
  550.0 2.2 reshape.732
  553.8 2.2 reshape.734
  (187 shorter events, 53.0 us)
Async XLA Ops:
  9.3 4.6 copy-start.32
  9.3 4.6 copy-start.33
  9.3 4.6 copy-start.34
  9.3 4.6 copy-start.35
  9.3 4.6 copy-start.36
  9.3 4.6 copy-start.37
  9.3 5.3 copy-start.6
  9.3 5.5 copy-start.29
  9.3 19.4 %all-to-all-start = ((bf16[4,36,3968]{2,1,0:T(8,128)(2,1)}), bf16[4,36,3968]{2,1,0:T(8,128)(2,1)S(1)}, u32[]{:S(2)}, u32[]{:S(2)}) async-start(bf16[4,36,3968]{2,1,0:T(8,128)(2,1)} %copy.124), calls=%async_computation | async-start | bytes 2539520 | tf_op jit(solution)/shard_map/all_to_all | solution.py:1038
  13.8 2.5 copy-start.24
  167.8 2.9 copy-start.2
  319.4 2.1 copy-start.1
  319.4 2.3 copy-start.5
  326.7 2.3 copy-start.10
  330.3 38.4 %copy-start.8 = (bf16[32,8,4,256]{3,1,2,0:T(8,128)(2,1)S(1)}, bf16[32,8,4,256]{3,1,2,0:T(8,128)(2,1)}, u32[]{:S(2)}) copy-start(bf16[32,8,4,256]{3,1,2,0:T(8,128)(2,1)} %copy-done.7) | copy-start | bytes 1572868
  366.1 2.6 copy-start.15
  368.7 2.3 copy-start.18
  373.9 4.0 copy-start.30
  388.0 2.0 copy-start.22
  388.0 2.0 copy-start.23
  517.6 11.8 %copy-start.19 = (f32[224,1152]{1,0:T(8,128)S(1)}, f32[224,1152]{1,0:T(8,128)}, u32[]{:S(2)}) copy-start(f32[224,1152]{1,0:T(8,128)} %get-tuple-element.59) | copy-start | bytes 3096580
  517.6 26.7 %all-to-all-start.1 = ((bf16[4,36,3968]{2,1,0:T(8,128)(2,1)}), bf16[4,36,3968]{2,1,0:T(8,128)(2,1)S(1)}, u32[]{:S(2)}, u32[]{:S(2)}) async-start(bf16[4,36,3968]{2,1,0:T(8,128)(2,1)} %reshape.729), calls=%async_computation.1 | async-start | bytes 2539520 | tf_op jit(solution)/shard_map/all_to_all | solution.py:1132
  553.7 2.2 copy-start.20
  553.7 3.0 copy-start.25
  (16 other events, 19.0 us)
